TPU v7x, 32 devices: a whole 2x2x4 slice. The times are simulated.
32 devices in a mesh: sky: 16 (over z, y, core), exp: 2 (over x).
Axes of the slice: x: 2, y: 2, z: 4, core: 2. Of those that a mesh axis runs over, the one named last changes fastest.
Arguments:
- warped: bfloat16 [4, 1920, 1024], P('exp', 'sky'), may hold values from -6 to 6
- variance: bfloat16 [4, 1920, 1024], P('exp', 'sky'), may hold values from 0.5 to 8
- basis_taps: bfloat16 [9, 2, 23], replicated, may hold values from -1.25 to 1.25
- coeffs: float32 [4, 9, 10], P('exp'), may hold values from -6 to 6
- degrees: int32 [4, 9], P('exp'), may hold values from 0 to 3
- footprint: int32 [4, 2], P('exp'), may hold values from 0 to 1920, as said below
- masks: int32 [4, 128], P('exp', 'sky'), may hold values from 0 to 1073741823
Outputs:
- coadd: float32 [1920, 1024], P('sky', 'exp')
Inputs may be any that keep to these rules, and one draw needn't show every extreme that they name: Each exposure covers rows footprint[e, 0] up to but not including footprint[e, 1], a nonempty range.
All inputs are finite; a program needn't handle non-finite values.
Results may differ from a plain program's by a relative error of at most 0.0039.
Values may be sent and summed in bfloat16 or wider, within the bound.
No kernel may reach another device: no remote copies, remote signals or barrier semaphores. Data moves between devices by JAX's collectives and lax.ppermute only.
A program may use at most 64 MiB of HBM per device.

v0:
```python
import jax
import jax.numpy as jnp
from jax import lax
from jax.sharding import PartitionSpec as P

HIGHEST = lax.Precision.HIGHEST
POWERS = ((0, 0), (1, 0), (0, 1), (2, 0), (1, 1), (0, 2), (3, 0), (2, 1), (1, 2), (0, 3))


def padded_2(cells, sides, width):
    for axis, dim in sides:
        count = lax.axis_size(axis)
        ends = count - 1
        head = lax.slice_in_dim(cells, 0, width, axis=dim)
        tail = lax.slice_in_dim(cells, cells.shape[dim] - width, cells.shape[dim], axis=dim)
        cells = jnp.concatenate(
            [
                lax.ppermute(tail, axis, [(i, (i + 1) % count) for i in range(ends)]),
                cells,
                lax.ppermute(head, axis, [((i + 1) % count, i) for i in range(ends)]),
            ],
            axis=dim,
        )
    return cells


def monomials(total_rows, total_cols, row_start, row_count):
    row_pos = (
        2.0 * (row_start + jnp.arange(row_count, dtype=jnp.int32)).astype(jnp.float32) + 1.0
    ) / total_rows - 1.0
    col_pos = (
        2.0 * jnp.arange(total_cols, dtype=jnp.int32).astype(jnp.float32) + 1.0
    ) / total_cols - 1.0
    return jnp.stack([(row_pos**p)[:, None] * (col_pos**q)[None, :] for p, q in POWERS])


def term_active(degree):
    orders = jnp.array([p + q for p, q in POWERS], dtype=jnp.int32)
    return (orders[None, :] <= degree[:, None]).astype(jnp.float32)


def pixel_weight(bounds, words, var_field, global_rows, local_rows):
    covered = ((global_rows >= bounds[0]) & (global_rows < bounds[1])).astype(jnp.float32)
    per_row = jnp.repeat(words, 15, total_repeat_length=local_rows.shape[0])
    offset = 2 * (local_rows % 15)
    lower = jnp.right_shift(per_row, offset) & 1
    upper = jnp.right_shift(per_row, offset + 1) & 1
    usable = (1 - lower * upper).astype(jnp.float32)
    return (covered * usable)[:, None] / var_field.astype(jnp.float32)


def body(warped, variance, basis_taps, coeffs, degrees, footprint, masks):
    exp_count, row_count, col_count = warped.shape
    basis_count = basis_taps.shape[0]
    tap_count = basis_taps.shape[2]
    half_width = tap_count // 2
    total_rows = row_count * lax.axis_size("sky")
    row_start = lax.axis_index("sky") * row_count
    strips = padded_2(warped, (("sky", 1),), half_width)
    tap_values = basis_taps.astype(jnp.float32)
    out_rows = jnp.arange(row_count, dtype=jnp.int32)[:, None]
    in_rows = jnp.arange(row_count + 2 * half_width, dtype=jnp.int32)[None, :]
    tap_index = jnp.arange(tap_count, dtype=jnp.int32)
    row_onehot = ((in_rows - out_rows)[:, :, None] == tap_index[None, None, :]).astype(jnp.float32)
    row_band = jnp.einsum("ihk,bk->bih", row_onehot, tap_values[:, 0, :], precision=HIGHEST).astype(
        jnp.bfloat16
    )
    window_pos = jnp.arange(256, dtype=jnp.int32)[:, None]
    block_pos = jnp.arange(128, dtype=jnp.int32)[None, :]
    col_onehot = (
        (window_pos - block_pos - 64 + half_width)[:, :, None] == tap_index[None, None, :]
    ).astype(jnp.float32)
    col_band = jnp.einsum("kcj,bj->bkc", col_onehot, tap_values[:, 1, :], precision=HIGHEST).astype(
        jnp.bfloat16
    )
    terms_field = monomials(total_rows, col_count, row_start, row_count)
    local_rows = jnp.arange(row_count, dtype=jnp.int32)
    global_rows = row_start + local_rows
    block_count = col_count // 128

    def first_pass(carry, item):
        image, coef, degree, bounds, words, var_field = item
        along_rows = jnp.einsum(
            "bih,hc->bic", row_band, image, preferred_element_type=jnp.float32
        ).astype(jnp.bfloat16)
        padded = jnp.pad(along_rows, ((0, 0), (0, 0), (64, 64))).reshape(
            basis_count, row_count, block_count + 1, 128
        )
        windows = jnp.concatenate([padded[:, :, :-1, :], padded[:, :, 1:, :]], axis=-1)
        along_cols = jnp.einsum(
            "brjk,bkc->brjc", windows, col_band, preferred_element_type=jnp.float32
        ).reshape(basis_count, row_count, col_count)
        field = jnp.einsum(
            "bt,trc->brc", coef * term_active(degree), terms_field, precision=HIGHEST
        )
        matched = jnp.sum(field * along_cols, axis=0).astype(jnp.bfloat16)
        weight = pixel_weight(bounds, words, var_field, global_rows, local_rows)
        values = matched.astype(jnp.float32)
        return ((carry[0] + weight * values, carry[1] + weight), (matched, weight))

    start = (
        jnp.zeros((row_count, col_count), jnp.float32),
        jnp.zeros((row_count, col_count), jnp.float32),
    )
    (num_first, den_first), (matched_all, weight_all) = lax.scan(
        first_pass, start, (strips, coeffs, degrees, footprint, masks, variance)
    )
    num_share, den_share = (
        lax.psum_scatter(num_first, "exp", scatter_dimension=1, tiled=True),
        lax.psum_scatter(den_first, "exp", scatter_dimension=1, tiled=True),
    )
    first = lax.all_gather(num_share / (1.0 + den_share), "exp", axis=1, tiled=True)
    values = matched_all.astype(jnp.float32)
    excess = values - first[None, :, :]
    robust = weight_all / (1.0 + excess * excess / (9.0 * variance.astype(jnp.float32)))
    num_final = jnp.sum(robust * values, axis=0)
    den_final = jnp.sum(robust, axis=0)
    num_part, den_part = (
        lax.psum_scatter(num_final, "exp", scatter_dimension=1, tiled=True),
        lax.psum_scatter(den_final, "exp", scatter_dimension=1, tiled=True),
    )
    return num_part / (1.0 + den_part)


def solution(mesh):
    in_specs = (
        P("exp", "sky", None),
        P("exp", "sky", None),
        P(),
        P("exp", None, None),
        P("exp", None),
        P("exp", None),
        P("exp", "sky"),
    )
    out_specs = P("sky", "exp")
    return jax.shard_map(body, mesh=mesh, in_specs=in_specs, out_specs=out_specs, check_vma=False)
```

profile of v0, /device:TPU:0, one launch (start us, length us, event | category | flops | bytes accessed | tf_op | source)
XLA Modules:
  0.0 220.5 jit_solution(5804931433698877517)
XLA Ops:
  7.4 2.4 %collective-permute-start = (bf16[2,11,1024]{2,1,0:T(8,128)(2,1)S(1)}, bf16[2,11,1024]{2,1,0:T(8,128)(2,1)S(1)}, u32[]{:S(2)}, u32[]{:S(2)}) collective-permute-start(bf16[2,11,1024]{2,1,0:T(8,128)(2,1)S(1)} %get-tuple-element.705), channel_id=1, source_target_pairs={{0,2},{2,4},{4,6},{6,8},{8,10},{10,12},{12,14},{14,16},{16,18},{18... | collective-permute-start | bytes 135176 | tf_op jit(solution)/shard_map/ppermute | solution.py:18
  9.8 1.3 collective-permute-start.1
  21.4 8.6 %copy.31 = f32[10,120,1024]{2,0,1:T(8,128)} copy(f32[10,120,1024]{2,1,0:T(8,128)} %broadcast_dynamic-update-slice_fusion) | data formatting | bytes 9830400
  30.0 1.0 copy.33
  31.8 1.0 pad_maximum_fusion
  32.9 99.8 %while.26 = (s32[]{:T(128)}, f32[120,1024]{1,0:T(8,128)S(1)}, f32[120,1024]{1,0:T(8,128)S(1)}, bf16[2,120,1024]{2,1,0:T(8,128)(2,1)}, f32[2,120,1024]{2,1,0:T(8,...) while((s32[]{:T(128)}, f32[120,1024]{1,0:T(8,128)S(1)}, ...), condition=%wide.region_2.3_spmd.clone.clone.clone, body=%wide.region_0.2_spmd.sunk.clone.clone.clone.sunk | while | flops 1026297152 | bytes 74979888 | solution.py:105
  34.4 6.2 %and_select_fusion.3 = f32[120]{0:T(128)S(1)} fusion(pred[120]{0:T(512)(128)(4,1)S(1)} %get-tuple-element.898, pred[120]{0:T(512)(128)(4,1)S(1)} %get-tuple-element.899, pred[120]{0:T(512)(128)(4,1)S(1)} %get-tuple-element.900, pred[120]{0:T(512)(128)(4,1)S(1)} %get-tuple-element.901, pred[120]{0:T(512)(128)(4,1)S(1)} %get-tuple-element.902, ...), kind=kLoop, calls=%fused_computation.32.clone.1 | loop fusion | flops 3240 | bytes 1364 | tf_op jit(solution)/shard_map/while/body/eval_jaxpr/mul | solution.py:49
  40.6 3.3 %convert_bitcast_fusion.3 = bf16[9,120,1024]{2,1,0:T(8,128)(2,1)} fusion(bf16[9,120,142]{1,2,0:T(8,128)(2,1)} %get-tuple-element.894, bf16[2,142,1024]{2,1,0:T(8,128)(2,1)} %get-tuple-element.893, s32[]{:T(128)} %get-tuple-element.856), kind=kOutput, calls=%fused_computation.8.clone.1 | convolution fusion | flops 315187200 | bytes 2839040 | tf_op jit(solution)/shard_map/while/body/eval_jaxpr/bih,hc->bic/dot_general | solution.py:83
  43.9 3.0 %copy.61 = bf16[9,120,1024]{1,2,0:T(8,128)(2,1)S(1)} copy(bf16[9,120,1024]{2,1,0:T(8,128)(2,1)} %convert_bitcast_fusion.3) | data formatting | bytes 4423680 | tf_op jit(solution)/shard_map/while
  47.5 2.6 %fusion.71 = (bf16[9,120,8,128]{1,3,2,0:T(8,128)(2,1)S(1)}, bf16[9,120,8,128]{1,3,2,0:T(8,128)(2,1)}) fusion(bf16[9,120,9,128]{1,3,2,0:T(8,128)(2,1)S(1)} %bitcast.102), kind=kLoop, calls=%fused_computation.80.clone.1 | loop fusion | bytes 8847360 | tf_op jit(solution)/shard_map/while/body/eval_jaxpr/slice | solution.py:89
  50.1 4.4 %copy.62 = bf16[9,120,8,128]{3,2,1,0:T(8,128)(2,1)} copy(bf16[9,120,8,128]{1,3,2,0:T(8,128)(2,1)} %get-tuple-element.826) | data formatting | bytes 4423680 | tf_op jit(solution)/shard_map/while
  54.5 2.6 %copy.63 = bf16[9,120,8,128]{3,2,1,0:T(8,128)(2,1)} copy(bf16[9,120,8,128]{1,3,2,0:T(8,128)(2,1)S(1)} %get-tuple-element.827) | data formatting | bytes 4423680 | tf_op jit(solution)/shard_map/while
  57.1 5.7 %fusion.72 = f32[9,120,8,128]{3,2,1,0:T(8,128)} fusion(bf16[9,120,8,128]{3,2,1,0:T(8,128)(2,1)} %copy.62, bf16[9,120,8,128]{3,2,1,0:T(8,128)(2,1)} %copy.63, bf16[9,256,128]{2,1,0:T(8,128)(2,1)} %get-tuple-element.895), kind=kOutput, calls=%fused_computation.4.clone.1 | convolution fusion | flops 575078400 | bytes 9437184 | tf_op jit(solution)/shard_map/while/body/eval_jaxpr/brjk,bkc->brjc/dot_general | solution.py:90
  62.8 5.5 %reshape.423 = f32[9,120,1024]{2,1,0:T(8,128)} reshape(f32[9,120,8,128]{3,2,1,0:T(8,128)} %fusion.72) | data formatting | bytes 8847360 | tf_op jit(solution)/shard_map/while/body/eval_jaxpr/reshape | solution.py:92
  68.3 13.1 %fusion.74 = bf16[120,1024]{1,0:T(8,128)(2,1)S(1)} fusion(f32[9,120,1024]{2,1,0:T(8,128)} %reshape.423, f32[10,120,1024]{2,0,1:T(8,128)} %get-tuple-element.892, f32[1,9,10]{2,0,1:T(1,128)S(1)} %constant_dynamic-slice_fusion.9, s32[10]{0:T(128)S(1)} %get-tuple-element.907, s32[9]{0:T(128)S(1)} %fusion.73), kind=kOutput, calls=%fused_computation.3.clone.1 | convolution fusion | flops 134799536 | bytes 9585076 | tf_op jit(solution)/shard_map/while/body/eval_jaxpr/bt,trc->brc/dot_general | solution.py:93
  84.2 6.2 %and_select_fusion.3 = f32[120]{0:T(128)S(1)} fusion(pred[120]{0:T(512)(128)(4,1)S(1)} %get-tuple-element.898, pred[120]{0:T(512)(128)(4,1)S(1)} %get-tuple-element.899, pred[120]{0:T(512)(128)(4,1)S(1)} %get-tuple-element.900, pred[120]{0:T(512)(128)(4,1)S(1)} %get-tuple-element.901, pred[120]{0:T(512)(128)(4,1)S(1)} %get-tuple-element.902, ...), kind=kLoop, calls=%fused_computation.32.clone.1 | loop fusion | flops 3240 | bytes 1364 | tf_op jit(solution)/shard_map/while/body/eval_jaxpr/mul | solution.py:49
  90.4 3.3 %convert_bitcast_fusion.3 = bf16[9,120,1024]{2,1,0:T(8,128)(2,1)} fusion(bf16[9,120,142]{1,2,0:T(8,128)(2,1)} %get-tuple-element.894, bf16[2,142,1024]{2,1,0:T(8,128)(2,1)} %get-tuple-element.893, s32[]{:T(128)} %get-tuple-element.856), kind=kOutput, calls=%fused_computation.8.clone.1 | convolution fusion | flops 315187200 | bytes 2839040 | tf_op jit(solution)/shard_map/while/body/eval_jaxpr/bih,hc->bic/dot_general | solution.py:83
  93.7 3.0 %copy.61 = bf16[9,120,1024]{1,2,0:T(8,128)(2,1)S(1)} copy(bf16[9,120,1024]{2,1,0:T(8,128)(2,1)} %convert_bitcast_fusion.3) | data formatting | bytes 4423680 | tf_op jit(solution)/shard_map/while
  97.3 2.6 %fusion.71 = (bf16[9,120,8,128]{1,3,2,0:T(8,128)(2,1)S(1)}, bf16[9,120,8,128]{1,3,2,0:T(8,128)(2,1)}) fusion(bf16[9,120,9,128]{1,3,2,0:T(8,128)(2,1)S(1)} %bitcast.102), kind=kLoop, calls=%fused_computation.80.clone.1 | loop fusion | bytes 8847360 | tf_op jit(solution)/shard_map/while/body/eval_jaxpr/slice | solution.py:89
  99.9 4.4 %copy.62 = bf16[9,120,8,128]{3,2,1,0:T(8,128)(2,1)} copy(bf16[9,120,8,128]{1,3,2,0:T(8,128)(2,1)} %get-tuple-element.826) | data formatting | bytes 4423680 | tf_op jit(solution)/shard_map/while
  104.3 2.6 %copy.63 = bf16[9,120,8,128]{3,2,1,0:T(8,128)(2,1)} copy(bf16[9,120,8,128]{1,3,2,0:T(8,128)(2,1)S(1)} %get-tuple-element.827) | data formatting | bytes 4423680 | tf_op jit(solution)/shard_map/while
  106.9 5.7 %fusion.72 = f32[9,120,8,128]{3,2,1,0:T(8,128)} fusion(bf16[9,120,8,128]{3,2,1,0:T(8,128)(2,1)} %copy.62, bf16[9,120,8,128]{3,2,1,0:T(8,128)(2,1)} %copy.63, bf16[9,256,128]{2,1,0:T(8,128)(2,1)} %get-tuple-element.895), kind=kOutput, calls=%fused_computation.4.clone.1 | convolution fusion | flops 575078400 | bytes 9437184 | tf_op jit(solution)/shard_map/while/body/eval_jaxpr/brjk,bkc->brjc/dot_general | solution.py:90
  112.6 5.5 %reshape.423 = f32[9,120,1024]{2,1,0:T(8,128)} reshape(f32[9,120,8,128]{3,2,1,0:T(8,128)} %fusion.72) | data formatting | bytes 8847360 | tf_op jit(solution)/shard_map/while/body/eval_jaxpr/reshape | solution.py:92
  118.1 13.1 %fusion.74 = bf16[120,1024]{1,0:T(8,128)(2,1)S(1)} fusion(f32[9,120,1024]{2,1,0:T(8,128)} %reshape.423, f32[10,120,1024]{2,0,1:T(8,128)} %get-tuple-element.892, f32[1,9,10]{2,0,1:T(1,128)S(1)} %constant_dynamic-slice_fusion.9, s32[10]{0:T(128)S(1)} %get-tuple-element.907, s32[9]{0:T(128)S(1)} %fusion.73), kind=kOutput, calls=%fused_computation.3.clone.1 | convolution fusion | flops 134799536 | bytes 9585076 | tf_op jit(solution)/shard_map/while/body/eval_jaxpr/bt,trc->brc/dot_general | solution.py:93
  134.3 18.2 %reduce-scatter.5.cloned.1.call-done = f32[120,512]{1,0:T(8,128)} async-done(((f32[120,1024]{1,0:T(8,128)}), f32[120,512]{1,0:T(8,128)}) %reduce-scatter.5.cloned.1.call-update) | async-done | bytes 245776 | tf_op jit(solution)/shard_map/reduce_scatter | solution.py:109
  152.5 16.5 %reduce-scatter.7.cloned.1.call-done = f32[120,512]{1,0:T(8,128)} async-done(((f32[120,1024]{1,0:T(8,128)}), f32[120,512]{1,0:T(8,128)}) %reduce-scatter.7.cloned.1.call-update) | async-done | bytes 245776 | tf_op jit(solution)/shard_map/reduce_scatter | solution.py:110
  169.0 1.1 add_divide_fusion.1
  170.1 8.4 %all_gather.3 = f32[120,1024]{1,0:T(8,128)S(1)} all-gather(f32[120,512]{1,0:T(8,128)S(1)} %add_divide_fusion.1), channel_id=1, replica_groups=mesh['sky'=16,'exp'=2] {'exp'}, dimensions={1}, use_global_device_ids=true | all-gather | bytes 737280 | tf_op jit(solution)/shard_map/all_gather | solution.py:112
  178.4 3.0 %fusion.42 = (f32[120,1024]{1,0:T(8,128)}, f32[120,1024]{1,0:T(8,128)}) fusion(bf16[2,120,1024]{2,1,0:T(8,128)(2,1)} %get-tuple-element.468, f32[2,120,1024]{2,1,0:T(8,128)} %get-tuple-element.467, bf16[2,120,1024]{2,1,0:T(8,128)(2,1)} %get-tuple-element.916, f32[120,1024]{1,0:T(8,128)S(1)} %all_gather.3), kind=kLoop, calls=%fused_computation.79 | loop fusion | flops 2457600 | bytes 3440640 | tf_op jit(solution)/shard_map/reduce_sum | solution.py:117
  182.1 13.8 %reduce-scatter.11.cloned.1.call-done = f32[120,512]{1,0:T(8,128)} async-done(((f32[120,1024]{1,0:T(8,128)}), f32[120,512]{1,0:T(8,128)}) %reduce-scatter.11.cloned.1.call-update) | async-done | bytes 245776 | tf_op jit(solution)/shard_map/reduce_scatter | solution.py:120
  195.9 16.3 %reduce-scatter.9.cloned.1.call-done = f32[120,512]{1,0:T(8,128)} async-done(((f32[120,1024]{1,0:T(8,128)}), f32[120,512]{1,0:T(8,128)}) %reduce-scatter.9.cloned.1.call-update) | async-done | bytes 245776 | tf_op jit(solution)/shard_map/reduce_scatter | solution.py:119
  212.2 1.8 add_divide_fusion
  (108 shorter events, 20.6 us)
Async XLA Ops:
  6.5 12.6 %copy-start.9 = (bf16[9,2,23]{2,1,0:T(2,128)(2,1)S(1)}, bf16[9,2,23]{2,1,0:T(2,128)(2,1)}, u32[]{:S(2)}) copy-start(bf16[9,2,23]{2,1,0:T(2,128)(2,1)} %param.14) | copy-start | bytes 2488
  6.5 145.9 %reduce-scatter.5.cloned.1.call-start = ((), (), s32[]{:S(2)}) async-start(), calls=%async_computation.4 | async-start | bytes 737280 | tf_op jit(solution)/shard_map/reduce_scatter | solution.py:109
  7.4 24.4 %collective-permute-start = (bf16[2,11,1024]{2,1,0:T(8,128)(2,1)S(1)}, bf16[2,11,1024]{2,1,0:T(8,128)(2,1)S(1)}, u32[]{:S(2)}, u32[]{:S(2)}) collective-permute-start(bf16[2,11,1024]{2,1,0:T(8,128)(2,1)S(1)} %get-tuple-element.705), channel_id=1, source_target_pairs={{0,2},{2,4},{4,6},{6,8},{8,10},{10,12},{12,14},{14,16},{16,18},{18... | collective-permute-start | bytes 135176 | tf_op jit(solution)/shard_map/ppermute | solution.py:18
  9.8 22.0 %collective-permute-start.1 = (bf16[2,11,1024]{2,1,0:T(8,128)(2,1)S(1)}, bf16[2,11,1024]{2,1,0:T(8,128)(2,1)S(1)}, u32[]{:S(2)}, u32[]{:S(2)}) collective-permute-start(bf16[2,11,1024]{2,1,0:T(8,128)(2,1)S(1)} %get-tuple-element.706), channel_id=1, source_target_pairs={{2,0},{4,2},{6,4},{8,6},{10,8},{12,10},{14,12},{16,14},{18,16},{20... | collective-permute-start | bytes 135176 | tf_op jit(solution)/shard_map/ppermute | solution.py:20
  21.2 10.6 %copy-start.5 = (bf16[2,120,1024]{2,1,0:T(8,128)(2,1)S(1)}, bf16[2,120,1024]{2,1,0:T(8,128)(2,1)}, u32[]{:S(2)}) copy-start(bf16[2,120,1024]{2,1,0:T(8,128)(2,1)} %param.12) | copy-start | bytes 1474564
  21.2 11.6 %copy-start.8 = (f32[2,9,10]{2,0,1:T(2,128)S(1)}, f32[2,9,10]{2,0,1:T(2,128)}, u32[]{:S(2)}) copy-start(f32[2,9,10]{2,0,1:T(2,128)} %param.15) | copy-start | bytes 2164
  21.2 11.6 %copy-start.10 = (s32[10]{0:T(128)S(1)}, s32[10]{0:T(128)}, u32[]{:S(2)}) copy-start(s32[10]{0:T(128)} %constant.260.clone..sunk.4) | copy-start | bytes 124
  21.3 11.6 %copy-start.11 = (pred[120]{0:T(512)(128)(4,1)S(1)}, pred[120]{0:T(512)(128)(4,1)}, u32[]{:S(2)}) copy-start(pred[120]{0:T(512)(128)(4,1)} %constant.373) | copy-start | bytes 364
  21.3 11.5 %copy-start.12 = (pred[120]{0:T(512)(128)(4,1)S(1)}, pred[120]{0:T(512)(128)(4,1)}, u32[]{:S(2)}) copy-start(pred[120]{0:T(512)(128)(4,1)} %constant.374) | copy-start | bytes 364
  21.3 11.5 %copy-start.13 = (pred[120]{0:T(512)(128)(4,1)S(1)}, pred[120]{0:T(512)(128)(4,1)}, u32[]{:S(2)}) copy-start(pred[120]{0:T(512)(128)(4,1)} %constant.375) | copy-start | bytes 364
  21.3 11.5 %copy-start.14 = (pred[120]{0:T(512)(128)(4,1)S(1)}, pred[120]{0:T(512)(128)(4,1)}, u32[]{:S(2)}) copy-start(pred[120]{0:T(512)(128)(4,1)} %constant.376) | copy-start | bytes 364
  21.3 11.5 %copy-start.15 = (pred[120]{0:T(512)(128)(4,1)S(1)}, pred[120]{0:T(512)(128)(4,1)}, u32[]{:S(2)}) copy-start(pred[120]{0:T(512)(128)(4,1)} %constant.377) | copy-start | bytes 364
  21.3 11.5 %copy-start.16 = (pred[120]{0:T(512)(128)(4,1)S(1)}, pred[120]{0:T(512)(128)(4,1)}, u32[]{:S(2)}) copy-start(pred[120]{0:T(512)(128)(4,1)} %constant.378) | copy-start | bytes 364
  21.3 11.5 %copy-start.17 = (pred[120]{0:T(512)(128)(4,1)S(1)}, pred[120]{0:T(512)(128)(4,1)}, u32[]{:S(2)}) copy-start(pred[120]{0:T(512)(128)(4,1)} %constant.379) | copy-start | bytes 364
  21.3 11.5 %copy-start.18 = (s32[2,2]{1,0:T(2,128)S(1)}, s32[2,2]{1,0:T(2,128)}, u32[]{:S(2)}) copy-start(s32[2,2]{1,0:T(2,128)} %param.17) | copy-start | bytes 52
  21.4 11.5 %copy-start.19 = (s32[2,8]{1,0:T(2,128)S(1)}, s32[2,8]{1,0:T(2,128)}, u32[]{:S(2)}) copy-start(s32[2,8]{1,0:T(2,128)} %param.18) | copy-start | bytes 196
  21.4 11.5 %copy-start.20 = (s32[2,9]{1,0:T(2,128)S(1)}, s32[2,9]{1,0:T(2,128)}, u32[]{:S(2)}) copy-start(s32[2,9]{1,0:T(2,128)} %param.16) | copy-start | bytes 220
  68.3 13.1 %copy-start.2 = (bf16[2,120,1024]{2,1,0:T(8,128)(2,1)S(1)}, bf16[2,120,1024]{2,1,0:T(8,128)(2,1)}, u32[]{:S(2)}) copy-start(bf16[2,120,1024]{2,1,0:T(8,128)(2,1)} %get-tuple-element.889) | copy-start | bytes 1474564 | tf_op jit(solution)/shard_map/while
  68.3 13.3 %copy-start.3 = (f32[2,120,1024]{2,1,0:T(8,128)S(1)}, f32[2,120,1024]{2,1,0:T(8,128)}, u32[]{:S(2)}) copy-start(f32[2,120,1024]{2,1,0:T(8,128)} %get-tuple-element.860) | copy-start | bytes 2949124 | tf_op jit(solution)/shard_map/while
  68.3 13.4 %copy-start.6 = (bf16[2,120,1024]{2,1,0:T(8,128)(2,1)S(1)}, bf16[2,120,1024]{2,1,0:T(8,128)(2,1)}, u32[]{:S(2)}) copy-start(bf16[2,120,1024]{2,1,0:T(8,128)(2,1)} %get-tuple-element.859) | copy-start | bytes 1474564 | tf_op jit(solution)/shard_map/while
  81.8 1.0 copy-start.4
  81.8 1.1 copy-start.7
  118.1 13.1 %copy-start.2 = (bf16[2,120,1024]{2,1,0:T(8,128)(2,1)S(1)}, bf16[2,120,1024]{2,1,0:T(8,128)(2,1)}, u32[]{:S(2)}) copy-start(bf16[2,120,1024]{2,1,0:T(8,128)(2,1)} %get-tuple-element.889) | copy-start | bytes 1474564 | tf_op jit(solution)/shard_map/while
  118.1 13.3 %copy-start.3 = (f32[2,120,1024]{2,1,0:T(8,128)S(1)}, f32[2,120,1024]{2,1,0:T(8,128)}, u32[]{:S(2)}) copy-start(f32[2,120,1024]{2,1,0:T(8,128)} %get-tuple-element.860) | copy-start | bytes 2949124 | tf_op jit(solution)/shard_map/while
  118.1 13.4 %copy-start.6 = (bf16[2,120,1024]{2,1,0:T(8,128)(2,1)S(1)}, bf16[2,120,1024]{2,1,0:T(8,128)(2,1)}, u32[]{:S(2)}) copy-start(bf16[2,120,1024]{2,1,0:T(8,128)(2,1)} %get-tuple-element.859) | copy-start | bytes 1474564 | tf_op jit(solution)/shard_map/while
  131.5 1.0 copy-start.4
  131.6 1.1 copy-start.7
  132.7 0.8 copy-start
  132.7 1.0 copy-start.1
  133.5 35.5 %reduce-scatter.7.cloned.1.call-start = ((), (), s32[]{:S(2)}) async-start(), calls=%async_computation.5 | async-start | bytes 737280 | tf_op jit(solution)/shard_map/reduce_scatter | solution.py:110
  134.2 61.6 %reduce-scatter.11.cloned.1.call-start = ((), (), s32[]{:S(2)}) async-start(), calls=%async_computation.7 | async-start | bytes 737280 | tf_op jit(solution)/shard_map/reduce_scatter | solution.py:120
  181.5 30.7 %reduce-scatter.9.cloned.1.call-start = ((), (), s32[]{:S(2)}) async-start(), calls=%async_computation.6 | async-start | bytes 737280 | tf_op jit(solution)/shard_map/reduce_scatter | solution.py:119
Sparse Core Ops, SparseCore 0:
  133.6 18.8 reduce-scatter.4
  154.7 14.1 reduce-scatter.6
  181.6 14.1 reduce-scatter.10
  198.0 14.1 reduce-scatter.8
where the time goes:
time: 222 us; the launch traced here: 221 us
  waiting for transfers between devices  65.9 us (30%)
  local copies, waits for them, and re-layouts  60.5 us (27%)
  matrix products  45.4 us (20%)
  other arithmetic  22.7 us (10%)
  between operations  13.4 us (6%)
  blocking collectives  8.38 us (4%)
  starting transfers between devices  3.78 us (2%)
    dot_general x2, matrix products, first_pass(): jnp.einsum('bt,trc->brc', coef * term_active(degree), terms_field, precis...  26.1 us
    while x26, local copies, waits for them, and re-layouts  22.1 us
    reduce_scatter x1, waiting for transfers between devices, body(): lax.psum_scatter(num_first, 'exp', scatter_dimension=1, tiled=True)  18.2 us
    unnamed x41, local copies, waits for them, and re-layouts  16.7 us
    reduce_scatter x1, waiting for transfers between devices, body(): lax.psum_scatter(den_first, 'exp', scatter_dimension=1, tiled=True)  16.5 us
    reduce_scatter x1, waiting for transfers between devices, body(): lax.psum_scatter(num_final, 'exp', scatter_dimension=1, tiled=True)  16.3 us
    reduce_scatter x1, waiting for transfers between devices, body(): lax.psum_scatter(den_final, 'exp', scatter_dimension=1, tiled=True)  13.8 us
    mul x2, other arithmetic, pixel_weight(): return (covered * usable)[:, None] / var_field.astype(jnp.float32)  12.4 us
  transfers between devices with their start and end apart: 6, of which 4 were waited for; matrix products, arithmetic and copies ran while one was open for 9% of the time, Pallas kernels for 0%

commit v1 on v0

v1 whole, which is shorter than its diff:
```python
import functools

import jax
import jax.numpy as jnp
from jax import lax
from jax.experimental import pallas as pl
from jax.experimental.pallas import tpu as pltpu
from jax.sharding import PartitionSpec as P

POWERS = ((0, 0), (1, 0), (0, 1), (2, 0), (1, 1), (0, 2), (3, 0), (2, 1), (1, 2), (0, 3))
TERM = {power: index for index, power in enumerate(POWERS)}
ROWS_PER_WORD = 15
EDGE = 16
WINDOW = 256
LANES = 128
PAD = 64
F32 = jnp.float32
BF16 = jnp.bfloat16


def round_up(value, unit):
    return -(-value // unit) * unit


def prep_kernel(width, shares, place, footprint, masks, variance, warped, tail, head, *masked):
    exp_count, row_count, col_count = variance.shape
    words = masks.shape[1]
    local = lax.broadcasted_iota(jnp.int32, (row_count, LANES), 0)
    total = local + place[0]
    for e in range(exp_count):
        image = warped[e].astype(F32)
        tail[e] = image[row_count - EDGE :].astype(BF16)
        head[e] = image[:EDGE].astype(BF16)
        word = jnp.full((row_count, LANES), masks[e, 0], jnp.int32)
        first = jnp.zeros((row_count, LANES), jnp.int32)
        for w in range(1, words):
            here = local >= w * ROWS_PER_WORD
            word = jnp.where(here, masks[e, w], word)
            first = jnp.where(here, w * ROWS_PER_WORD, first)
        planes = lax.shift_right_logical(word, 2 * (local - first)) & 3
        counts = (total >= footprint[e, 0]) & (total < footprint[e, 1]) & (planes != 3)
        for k in range(shares):
            start = pl.multiple_of(place[1 + k], LANES)
            for j in range(width // LANES):
                block = variance[e, :, pl.ds(pl.multiple_of(start + j * LANES, LANES), LANES)].astype(F32)
                masked[k][e, :, j * LANES : (j + 1) * LANES] = jnp.where(counts, block, jnp.inf).astype(BF16)


def band_kernel(taps, row_band, col_band):
    basis_count, _, tap_count = taps.shape
    half = tap_count // 2
    for b in range(basis_count):
        both = taps[b].astype(F32)
        both = jnp.concatenate([both, jnp.zeros((2, WINDOW - tap_count), F32)], axis=1)
        row_line = jnp.broadcast_to(pltpu.roll(both, WINDOW - half, 1)[0:1], (LANES, WINDOW))
        col_line = jnp.broadcast_to(pltpu.roll(both, PAD - half, 1)[1:2], (LANES, WINDOW))
        row_band[b] = pltpu.roll(row_line, 0, 1, stride=1, stride_axis=0).astype(BF16)
        col_band[b] = pltpu.roll(col_line, 0, 1, stride=1, stride_axis=0).T.astype(BF16)


def match_kernel(share, total_rows, place, coeffs, degrees, warped, above, below, row_band, col_band, matched, strip, rows, total):
    exp_count, row_count, col_count = warped.shape
    basis_count = row_band.shape[0]
    width = matched.shape[2]
    blocks = width // LANES
    start = pl.multiple_of(place[1 + share], LANES)
    left_at = pl.multiple_of(jnp.maximum(start - LANES, 0), LANES)
    right_at = pl.multiple_of(jnp.minimum(start + width, col_count - LANES), LANES)
    has_left = start > 0
    has_right = start + width < col_count

    def rows_of(e, at, size):
        middle = warped[e, :, pl.ds(at, size)].astype(F32)
        up = above[e, :, pl.ds(at, size)].astype(F32)
        down = below[e, :, pl.ds(at, size)].astype(F32)
        gap = jnp.zeros((WINDOW - row_count - 2 * EDGE, size), F32)
        return jnp.concatenate([middle, down, gap, up], axis=0)

    for e in range(exp_count):
        left = jnp.where(has_left, rows_of(e, left_at, LANES), 0.0)
        right = jnp.where(has_right, rows_of(e, right_at, LANES), 0.0)
        wide = jnp.concatenate([left, rows_of(e, start, width), right], axis=1)
        strip[e] = wide[:, PAD : PAD + width + LANES].astype(BF16)

    band = row_band[...].reshape(basis_count * LANES, WINDOW)
    for e in range(exp_count):
        rows[e] = jnp.dot(band, strip[e], preferred_element_type=F32).astype(BF16)

    row_at = place[0] + lax.broadcasted_iota(jnp.int32, (row_count, LANES), 0)
    u = (2.0 * row_at.astype(F32) + 1.0) / total_rows - 1.0
    total[...] = jnp.zeros_like(total)

    def one_basis(b, carry):
        columns = col_band[b]
        at = pl.multiple_of(b * LANES, LANES)
        for e in range(exp_count):
            degree = degrees[e, b]

            def term(p, q):
                return jnp.where(degree >= p + q, coeffs[e, b, TERM[p, q]], 0.0)

            a0 = term(0, 0) + u * (term(1, 0) + u * (term(2, 0) + u * term(3, 0)))
            a1 = term(0, 1) + u * (term(1, 1) + u * term(2, 1))
            a2 = term(0, 2) + u * term(1, 2)
            a3 = term(0, 3)
            for j in range(blocks):
                window = rows[e, pl.ds(at, LANES), j * LANES : j * LANES + WINDOW]
                along = jnp.dot(window, columns, preferred_element_type=F32)[:row_count]
                col_at = start + j * LANES + lax.broadcasted_iota(jnp.int32, (1, LANES), 1)
                v = (2.0 * col_at.astype(F32) + 1.0) / col_count - 1.0
                field = a0 + v * (a1 + v * (a2 + v * a3))
                total[e, :, j * LANES : (j + 1) * LANES] += field * along
        return carry

    lax.fori_loop(0, basis_count, one_basis, 0)
    matched[...] = total[...].astype(BF16)


def coadd_kernel(shares, *refs):
    fields, variances, coadd = refs[:shares], refs[shares : 2 * shares], refs[2 * shares]
    exp_count, row_count, width = fields[0].shape
    for j in range(width // LANES):
        span = slice(j * LANES, (j + 1) * LANES)
        values = [f[e, :, span].astype(F32) for f in fields for e in range(exp_count)]
        spreads = [s[e, :, span].astype(F32) for s in variances for e in range(exp_count)]
        weights = [1.0 / s for s in spreads]
        first = sum(w * x for w, x in zip(weights, values)) / (1.0 + sum(weights))
        robust = [1.0 / (s + (x - first) * (x - first) * (1.0 / 9.0)) for s, x in zip(spreads, values)]
        coadd[:, span] = sum(r * x for r, x in zip(robust, values)) / (1.0 + sum(robust))


def body(warped, variance, basis_taps, coeffs, degrees, footprint, masks):
    exp_count, row_count, col_count = warped.shape
    basis_count, _, tap_count = basis_taps.shape
    sky_count, shares = lax.axis_size("sky"), lax.axis_size("exp")
    width = col_count // shares
    total_rows = row_count * sky_count
    mine = lax.axis_index("exp")
    place = jnp.stack(
        [lax.axis_index("sky") * row_count] + [lax.rem(mine + k, shares) * width for k in range(shares)]
    ).astype(jnp.int32)
    smem = pl.BlockSpec(memory_space=pltpu.SMEM)
    vmem = pl.BlockSpec(memory_space=pltpu.VMEM)
    edge = jax.ShapeDtypeStruct((exp_count, EDGE, col_count), BF16)
    share = jax.ShapeDtypeStruct((exp_count, row_count, width), BF16)

    tail, head, *masked = pl.pallas_call(
        functools.partial(prep_kernel, width, shares),
        out_shape=[edge, edge] + [share] * shares,
        in_specs=[smem, smem, smem, vmem, vmem],
        out_specs=[vmem] * (2 + shares),
        name="prep",
    )(place, footprint, masks, variance, warped)

    def to_share(values, k):
        return lax.ppermute(values, "exp", [(i, (i + k) % shares) for i in range(shares)])

    spreads = [masked[0]] + [to_share(masked[k], k) for k in range(1, shares)]
    above = lax.ppermute(tail, "sky", [(i, i + 1) for i in range(sky_count - 1)])
    below = lax.ppermute(head, "sky", [(i + 1, i) for i in range(sky_count - 1)])

    row_band, col_band = pl.pallas_call(
        band_kernel,
        out_shape=[
            jax.ShapeDtypeStruct((basis_count, LANES, WINDOW), BF16),
            jax.ShapeDtypeStruct((basis_count, WINDOW, LANES), BF16),
        ],
        in_specs=[vmem],
        out_specs=[vmem, vmem],
        name="bands",
    )(basis_taps)

    def match(k):
        return pl.pallas_call(
            functools.partial(match_kernel, k, total_rows),
            out_shape=share,
            in_specs=[smem, smem, smem] + [vmem] * 5,
            out_specs=vmem,
            scratch_shapes=[
                pltpu.VMEM((exp_count, WINDOW, width + LANES), BF16),
                pltpu.VMEM((exp_count, basis_count * LANES, width + LANES), BF16),
                pltpu.VMEM((exp_count, row_count, width), F32),
            ],
            name="match",
        )(place, coeffs, degrees, warped, above, below, row_band, col_band)

    fields = [None] + [to_share(match(k), k) for k in range(1, shares)]
    fields[0] = match(0)

    return pl.pallas_call(
        functools.partial(coadd_kernel, shares),
        out_shape=jax.ShapeDtypeStruct((row_count, width), F32),
        in_specs=[vmem] * (2 * shares),
        out_specs=vmem,
        name="coadd",
    )(*fields, *spreads)


def solution(mesh):
    in_specs = (
        P("exp", "sky", None),
        P("exp", "sky", None),
        P(),
        P("exp", None, None),
        P("exp", None),
        P("exp", None),
        P("exp", "sky"),
    )
    return jax.shard_map(body, mesh=mesh, in_specs=in_specs, out_specs=P("sky", "exp"), check_vma=False)
```

time: 222 us -> 31.7 us (0.14)
  the two profiles are of different devices: /device:TPU:0 before, /device:TPU:23 now
where the time goes in v1:
time: 31.7 us; the launch traced here: 31.4 us
  Pallas kernels  19.6 us (62%)
  starting transfers between devices  6.26 us (20%)
  waiting for transfers between devices  2.98 us (9%)
  local copies, waits for them, and re-layouts  1.92 us (6%)
  other arithmetic  0.65 us (2%)
    pallas_call x2, Pallas kernels, match(): pl.pallas_call(functools.partial(match_kernel, k, total_rows), out_shape=...  12.6 us
    ppermute x1, starting transfers between devices, body(): lax.ppermute(tail, 'sky', [(i, i + 1) for i in range(sky_count - 1)])  3.7 us
    pallas_call x1, Pallas kernels, body(): pl.pallas_call(functools.partial(coadd_kernel, shares), out_shape=jax.Sha...  2.51 us
    pallas_call x1, Pallas kernels, body(): pl.pallas_call(band_kernel, out_shape=[jax.ShapeDtypeStruct((basis_count,...  2.37 us
    pallas_call x1, Pallas kernels, body(): pl.pallas_call(functools.partial(prep_kernel, width, shares), out_shape=[...  2.11 us
    ppermute x1, starting transfers between devices, body(): lax.ppermute(head, 'sky', [(i + 1, i) for i in range(sky_count - 1)])  1.92 us
    unnamed x11, local copies, waits for them, and re-layouts  1.92 us
    ppermute x2, waiting for transfers between devices, to_share(): lax.ppermute(values, 'exp', [(i, (i + k) % shares) for i in range(shares)])  1.51 us
  transfers between devices with their start and end apart: 4, of which 2 were waited for; matrix products, arithmetic and copies ran while one was open for 2% of the time, Pallas kernels for 48%

profile of v1, /device:TPU:23, one launch (start us, length us, event | category | flops | bytes accessed | tf_op | source)
XLA Modules:
  0.0 31.4 jit_solution(17867507668852145195)
XLA Ops:
  0.0 0.7 %pad_add_fusion.place = s32[3]{0:T(128)} fusion(s32[1]{0:T(128)} %bitcast.2, s32[1]{0:T(128)} %bitcast.1, s32[1]{0:T(128)} %bitcast), kind=kLoop, calls=%fused_computation | loop fusion | flops 6 | bytes 24 | tf_op jit(solution)/shard_map/stack | solution.py:139
  0.7 0.0 copy-start.4
  0.7 2.1 %prep.1 = (bf16[2,16,1024]{2,1,0:T(8,128)(2,1)}, bf16[2,16,1024]{2,1,0:T(8,128)(2,1)}, bf16[2,120,512]{2,1,0:T(8,128)(2,1)}, bf16[2,120,512]{2,1,0:T(8,128)(2,1)}) custom-call(s32[3]{0:T(128)} %pad_add_fusion.place, s32[2,2]{1,0:T(2,128)} %footprint.1, s32[2,8]{1,0:T(2,128)} %masks.1, bf16[2,120,1024]{2,1,0:T(8,128)(2,1)} %variance.1, ...), custom_call_target="tpu_custom_call" | custom-call | tf_op jit(solution)/shard_map/prep/pallas_call | solution.py:147
  2.8 3.7 %collective-permute-start = (bf16[2,16,1024]{2,1,0:T(8,128)(2,1)}, bf16[2,16,1024]{2,1,0:T(8,128)(2,1)S(1)}, u32[]{:S(2)}, u32[]{:S(2)}) collective-permute-start(bf16[2,16,1024]{2,1,0:T(8,128)(2,1)} %get-tuple-element.11), channel_id=1, source_target_pairs={{0,2},{2,4},{4,6},{6,8},{8,10},{10,12},{12,14},{14,16},{16,18},{18... | collective-permute-start | bytes 196616 | tf_op jit(solution)/shard_map/ppermute | solution.py:159
  6.5 1.9 %collective-permute-start.1 = (bf16[2,16,1024]{2,1,0:T(8,128)(2,1)}, bf16[2,16,1024]{2,1,0:T(8,128)(2,1)S(1)}, u32[]{:S(2)}, u32[]{:S(2)}) collective-permute-start(bf16[2,16,1024]{2,1,0:T(8,128)(2,1)} %get-tuple-element.12), channel_id=1, source_target_pairs={{2,0},{4,2},{6,4},{8,6},{10,8},{12,10},{14,12},{16,14},{18,16},{20... | collective-permute-start | bytes 196616 | tf_op jit(solution)/shard_map/ppermute | solution.py:160
  8.4 0.3 %collective-permute-start.3 = (bf16[2,120,512]{2,1,0:T(8,128)(2,1)}, bf16[2,120,512]{2,1,0:T(8,128)(2,1)S(1)}, u32[]{:S(2)}, u32[]{:S(2)}) collective-permute-start(bf16[2,120,512]{2,1,0:T(8,128)(2,1)} %get-tuple-element.16), channel_id=1, source_target_pairs={{0,1},{1,0},{2,3},{3,2},{4,5},{5,4},{6,7},{7,6},{8,9},{9,8},{10,11... | collective-permute-start | bytes 737288 | tf_op jit(solution)/shard_map/ppermute | solution.py:156
  8.7 0.0 copy-done.4
  8.7 0.6 %copy.8.coeffs = f32[2,9,10]{2,1,0:T(8,128)} copy(f32[2,9,10]{2,0,1:T(2,128)S(1)} %copy-done.4) | data formatting | bytes 1440 | tf_op args[3]
  9.3 2.4 %bands.1 = (bf16[9,128,256]{2,1,0:T(8,128)(2,1)}, bf16[9,256,128]{2,1,0:T(8,128)(2,1)}) custom-call(bf16[9,2,23]{2,1,0:T(2,128)(2,1)} %taps.1), custom_call_target="tpu_custom_call" | custom-call | tf_op jit(solution)/shard_map/bands/pallas_call | solution.py:162
  11.7 0.0 collective-permute-done.above
  11.7 0.0 copy-start
  11.7 1.5 %collective-permute-done.1.below = bf16[2,16,1024]{2,1,0:T(8,128)(2,1)S(1)} collective-permute-done((bf16[2,16,1024]{2,1,0:T(8,128)(2,1)}, bf16[2,16,1024]{2,1,0:T(8,128)(2,1)S(1)}, u32[]{:S(2)}, u32[]{:S(2)}) %collective-permute-start.1) | collective-permute-done | bytes 65568 | tf_op jit(solution)/shard_map/ppermute | solution.py:160
  13.2 0.0 copy-start.1
  13.2 0.0 copy-done
  13.2 0.6 %copy-done.1 = bf16[2,16,1024]{2,1,0:T(8,128)(2,1)} copy-done((bf16[2,16,1024]{2,1,0:T(8,128)(2,1)}, bf16[2,16,1024]{2,1,0:T(8,128)(2,1)S(1)}, u32[]{:S(2)}) %copy-start.1) | copy-done | bytes 65560
  13.8 6.3 %match.3 = bf16[2,120,512]{2,1,0:T(8,128)(2,1)} custom-call(s32[3]{0:T(128)} %pad_add_fusion.place, f32[2,9,10]{2,1,0:T(8,128)} %copy.8.coeffs, s32[2,9]{1,0:T(2,128)} %degrees.3, bf16[2,120,1024]{2,1,0:T(8,128)(2,1)} %warped.5, bf16[2,16,1024]{2,1,0:T(8,128)(2,1)} %copy-done, bf16[2,16,1024]{2,1,0:T(8,128)(2,1)} %copy-done.1, ...), custom_call_target="tpu_custom_call" | custom-call | tf_op jit(solution)/shard_map/match/pallas_call | solution.py:174
  20.0 0.3 %collective-permute-start.2 = (bf16[2,120,512]{2,1,0:T(8,128)(2,1)}, bf16[2,120,512]{2,1,0:T(8,128)(2,1)S(1)}, u32[]{:S(2)}, u32[]{:S(2)}) collective-permute-start(bf16[2,120,512]{2,1,0:T(8,128)(2,1)} %match.3), channel_id=1, source_target_pairs={{0,1},{1,0},{2,3},{3,2},{4,5},{5,4},{6,7},{7,6},{8,9},{9,8},{10,11... | collective-permute-start | bytes 737288 | tf_op jit(solution)/shard_map/ppermute | solution.py:156
  20.4 6.3 %match.2.refs_0_ = bf16[2,120,512]{2,1,0:T(8,128)(2,1)} custom-call(s32[3]{0:T(128)} %pad_add_fusion.place, f32[2,9,10]{2,1,0:T(8,128)} %copy.8.coeffs, s32[2,9]{1,0:T(2,128)} %degrees.3, bf16[2,120,1024]{2,1,0:T(8,128)(2,1)} %warped.5, bf16[2,16,1024]{2,1,0:T(8,128)(2,1)} %copy-done, bf16[2,16,1024]{2,1,0:T(8,128)(2,1)} %copy-done.1, ...), custom_call_target="tpu_custom_call" | custom-call | tf_op jit(solution)/shard_map/match/pallas_call | solution.py:174
  26.7 0.0 collective-permute-done.3.refs_3_
  26.7 0.0 copy-start.2
  26.7 1.5 %collective-permute-done.2.refs_1_ = bf16[2,120,512]{2,1,0:T(8,128)(2,1)S(1)} collective-permute-done((bf16[2,120,512]{2,1,0:T(8,128)(2,1)}, bf16[2,120,512]{2,1,0:T(8,128)(2,1)S(1)}, u32[]{:S(2)}, u32[]{:S(2)}) %collective-permute-start.2) | collective-permute-done | bytes 245792 | tf_op jit(solution)/shard_map/ppermute | solution.py:156
  28.2 0.0 copy-start.3
  28.2 0.0 copy-done.2
  28.2 0.7 %copy-done.3 = bf16[2,120,512]{2,1,0:T(8,128)(2,1)} copy-done((bf16[2,120,512]{2,1,0:T(8,128)(2,1)}, bf16[2,120,512]{2,1,0:T(8,128)(2,1)S(1)}, u32[]{:S(2)}) %copy-start.3) | copy-done | bytes 245784
  28.9 2.5 %coadd.1 = f32[120,512]{1,0:T(8,128)} custom-call(bf16[2,120,512]{2,1,0:T(8,128)(2,1)} %match.2.refs_0_, bf16[2,120,512]{2,1,0:T(8,128)(2,1)} %copy-done.3, bf16[2,120,512]{2,1,0:T(8,128)(2,1)} %get-tuple-element.15.refs_2_, bf16[2,120,512]{2,1,0:T(8,128)(2,1)} %copy-done.2), custom_call_target="tpu_custom_call" | custom-call | tf_op jit(solution)/shard_map/coadd/pallas_call | solution.py:190
Async XLA Ops:
  0.7 8.1 %copy-start.4 = (f32[2,9,10]{2,0,1:T(2,128)S(1)}, f32[2,9,10]{2,0,1:T(2,128)}, u32[]{:S(2)}) copy-start(f32[2,9,10]{2,0,1:T(2,128)} %param.10) | copy-start | bytes 2164
  2.8 8.9 %collective-permute-start = (bf16[2,16,1024]{2,1,0:T(8,128)(2,1)}, bf16[2,16,1024]{2,1,0:T(8,128)(2,1)S(1)}, u32[]{:S(2)}, u32[]{:S(2)}) collective-permute-start(bf16[2,16,1024]{2,1,0:T(8,128)(2,1)} %get-tuple-element.11), channel_id=1, source_target_pairs={{0,2},{2,4},{4,6},{6,8},{8,10},{10,12},{12,14},{14,16},{16,18},{18... | collective-permute-start | bytes 196616 | tf_op jit(solution)/shard_map/ppermute | solution.py:159
  6.5 6.7 %collective-permute-start.1 = (bf16[2,16,1024]{2,1,0:T(8,128)(2,1)}, bf16[2,16,1024]{2,1,0:T(8,128)(2,1)S(1)}, u32[]{:S(2)}, u32[]{:S(2)}) collective-permute-start(bf16[2,16,1024]{2,1,0:T(8,128)(2,1)} %get-tuple-element.12), channel_id=1, source_target_pairs={{2,0},{4,2},{6,4},{8,6},{10,8},{12,10},{14,12},{16,14},{18,16},{20... | collective-permute-start | bytes 196616 | tf_op jit(solution)/shard_map/ppermute | solution.py:160
  8.4 18.3 %collective-permute-start.3 = (bf16[2,120,512]{2,1,0:T(8,128)(2,1)}, bf16[2,120,512]{2,1,0:T(8,128)(2,1)S(1)}, u32[]{:S(2)}, u32[]{:S(2)}) collective-permute-start(bf16[2,120,512]{2,1,0:T(8,128)(2,1)} %get-tuple-element.16), channel_id=1, source_target_pairs={{0,1},{1,0},{2,3},{3,2},{4,5},{5,4},{6,7},{7,6},{8,9},{9,8},{10,11... | collective-permute-start | bytes 737288 | tf_op jit(solution)/shard_map/ppermute | solution.py:156
  11.7 1.5 %copy-start = (bf16[2,16,1024]{2,1,0:T(8,128)(2,1)}, bf16[2,16,1024]{2,1,0:T(8,128)(2,1)S(1)}, u32[]{:S(2)}) copy-start(bf16[2,16,1024]{2,1,0:T(8,128)(2,1)S(1)} %collective-permute-done.above) | copy-start | bytes 196612
  13.2 0.6 %copy-start.1 = (bf16[2,16,1024]{2,1,0:T(8,128)(2,1)}, bf16[2,16,1024]{2,1,0:T(8,128)(2,1)S(1)}, u32[]{:S(2)}) copy-start(bf16[2,16,1024]{2,1,0:T(8,128)(2,1)S(1)} %collective-permute-done.1.below) | copy-start | bytes 196612
  20.0 8.2 %collective-permute-start.2 = (bf16[2,120,512]{2,1,0:T(8,128)(2,1)}, bf16[2,120,512]{2,1,0:T(8,128)(2,1)S(1)}, u32[]{:S(2)}, u32[]{:S(2)}) collective-permute-start(bf16[2,120,512]{2,1,0:T(8,128)(2,1)} %match.3), channel_id=1, source_target_pairs={{0,1},{1,0},{2,3},{3,2},{4,5},{5,4},{6,7},{7,6},{8,9},{9,8},{10,11... | collective-permute-start | bytes 737288 | tf_op jit(solution)/shard_map/ppermute | solution.py:156
  26.7 1.5 %copy-start.2 = (bf16[2,120,512]{2,1,0:T(8,128)(2,1)}, bf16[2,120,512]{2,1,0:T(8,128)(2,1)S(1)}, u32[]{:S(2)}) copy-start(bf16[2,120,512]{2,1,0:T(8,128)(2,1)S(1)} %collective-permute-done.3.refs_3_) | copy-start | bytes 737284
  28.2 0.7 %copy-start.3 = (bf16[2,120,512]{2,1,0:T(8,128)(2,1)}, bf16[2,120,512]{2,1,0:T(8,128)(2,1)S(1)}, u32[]{:S(2)}) copy-start(bf16[2,120,512]{2,1,0:T(8,128)(2,1)S(1)} %collective-permute-done.2.refs_1_) | copy-start | bytes 737284

commit v2 on v1

v2 whole, which is shorter than its diff:
```python
import functools

import jax
import jax.numpy as jnp
from jax import lax
from jax.experimental import pallas as pl
from jax.experimental.pallas import tpu as pltpu
from jax.sharding import PartitionSpec as P

POWERS = ((0, 0), (1, 0), (0, 1), (2, 0), (1, 1), (0, 2), (3, 0), (2, 1), (1, 2), (0, 3))
TERM = {power: index for index, power in enumerate(POWERS)}
ROWS_PER_WORD = 15
EDGE = 16
LANES = 128
GROUP = 1
F32 = jnp.float32
BF16 = jnp.bfloat16


def round_up(value, unit):
    return -(-value // unit) * unit


def segments(width, tap_count):
    valid = LANES - tap_count + 1
    return [(at, min(valid, width - at)) for at in range(0, width, valid)]


def share_start(k, shares, width):
    return pl.multiple_of(lax.rem(lax.axis_index("exp") + k, shares) * width, LANES)


def variance_kernel(variance, *parts):
    shares, width = len(parts), parts[0].shape[2]
    for k in range(shares):
        parts[k][...] = variance[:, :, pl.ds(share_start(k, shares, width), width)]


def edges_kernel(warped, near, far):
    row_count = warped.shape[1]
    even = lax.rem(lax.axis_index("sky"), 2) == 0
    for e in range(warped.shape[0]):
        image = warped[e].astype(F32)
        head, tail = image[:EDGE], image[row_count - EDGE :]
        near[e] = jnp.where(even, tail, head).astype(BF16)
        far[e] = jnp.where(even, head, tail).astype(BF16)


def setup_kernel(taps, coeffs, degrees, footprint, masks, inner_band, outer_band, col_band, active, covered):
    basis_count, _, tap_count = taps.shape
    exp_count, row_count, _ = covered.shape
    half = tap_count // 2
    inner = inner_band.shape[1]

    both = jnp.concatenate([taps[b].astype(F32) for b in range(basis_count)], axis=0)
    lines = jnp.concatenate([both, jnp.zeros((2 * basis_count, LANES - tap_count), F32)], axis=1).astype(BF16)
    lane = lax.broadcasted_iota(jnp.int32, (LANES, LANES), 1)
    tap = lax.broadcasted_iota(jnp.int32, (LANES, LANES), 0)
    flip = (lane + tap == LANES).astype(F32) + ((lane == 0) & (tap == 0)).astype(F32)
    flipped = jnp.dot(lines, flip.astype(BF16), preferred_element_type=F32)
    lines = lines.astype(F32)

    def circulant(line, size):
        return pltpu.roll(jnp.broadcast_to(line, (size, LANES)), 0, 1, stride=1, stride_axis=0)

    near = pltpu.roll(lines, EDGE - half, 1)
    far = pltpu.roll(lines, LANES - 2 * EDGE - half, 1)
    for b in range(basis_count):
        upper = circulant(near[2 * b : 2 * b + 1], inner)
        lower = circulant(far[2 * b : 2 * b + 1], EDGE)
        inner_band[b] = upper.astype(BF16)
        outer_band[b] = jnp.concatenate([upper[:EDGE], lower], axis=0).astype(BF16)
        col_band[b] = circulant(flipped[2 * b + 1 : 2 * b + 2], LANES).astype(BF16)

    term_count = coeffs.shape[2]
    term = lax.broadcasted_iota(jnp.int32, (1, term_count), 1)
    order = jnp.zeros((1, term_count), F32)
    for index, (p, q) in enumerate(POWERS):
        order = jnp.where(term == index, float(p + q), order)
    wide = jnp.concatenate([degrees[...].astype(F32), jnp.zeros((exp_count, LANES - basis_count), F32)], axis=1)
    by_basis = jnp.concatenate([wide, jnp.zeros((8 - exp_count, LANES), F32)], axis=0).T
    local = lax.broadcasted_iota(jnp.int32, (row_count, LANES), 0)
    total = local + lax.axis_index("sky") * row_count
    for e in range(exp_count):
        own = jnp.concatenate([coeffs[b, e : e + 1, :] for b in range(basis_count)], axis=0)
        kept = jnp.where(order <= by_basis[:basis_count, e : e + 1], own, 0.0)
        kept = jnp.concatenate([kept, jnp.zeros((16 - basis_count, term_count), F32)], axis=0)
        active[e] = jnp.concatenate([kept, jnp.zeros((16, LANES - term_count), F32)], axis=1)
        word = jnp.broadcast_to(masks[e : e + 1, 0:1], (row_count, LANES))
        first = jnp.zeros((row_count, LANES), jnp.int32)
        for w in range(1, masks.shape[1]):
            here = local >= w * ROWS_PER_WORD
            word = jnp.where(here, jnp.broadcast_to(masks[e : e + 1, w : w + 1], (row_count, LANES)), word)
            first = jnp.where(here, w * ROWS_PER_WORD, first)
        planes = lax.shift_right_logical(word, 2 * (local - first)) & 3
        low = jnp.broadcast_to(footprint[e : e + 1, 0:1], (row_count, LANES))
        high = jnp.broadcast_to(footprint[e : e + 1, 1:2], (row_count, LANES))
        covered[e] = ((total >= low) & (total < high) & (planes != 3)).astype(F32)


def windows_of(read, start, width, col_count, parts, half):
    left_at = pl.multiple_of(jnp.maximum(start - LANES, 0), LANES)
    right_at = pl.multiple_of(jnp.minimum(start + width, col_count - LANES), LANES)
    left = jnp.where(start > 0, read(left_at, LANES), 0.0)
    right = jnp.where(start + width < col_count, read(right_at, LANES), 0.0)
    middle = read(start, width)
    blocks = [left] + [middle[:, at : at + LANES] for at in range(0, width, LANES)] + [right]
    blocks = [pltpu.roll(block, half, 1) for block in blocks]
    lane = lax.broadcasted_iota(jnp.int32, left.shape, 1)
    place = jnp.where(lane >= half, lane - half, lane - half + LANES)
    pieces = []
    for at, _ in parts:
        base, offset = divmod(LANES + at - half, LANES)
        pieces.append(jnp.where(place >= offset, blocks[base], blocks[base + 1]))
    return jnp.concatenate(pieces, axis=1).astype(BF16)


def line_polynomials(active, lines, start, parts, col_count):
    exp_count = active.shape[0]
    for e in range(exp_count):
        values = active[e]

        def column(p, q):
            return jnp.broadcast_to(values[:, TERM[p, q] : TERM[p, q] + 1], values.shape)

        for s, (at, size) in enumerate(parts):
            lane = lax.broadcasted_iota(jnp.int32, values.shape, 1)
            col_at = at + jnp.where(lane >= at % LANES, lane - at % LANES, lane - at % LANES + LANES)
            v = (2.0 * (start + col_at).astype(F32) + 1.0) / col_count - 1.0
            span = slice(s * LANES, (s + 1) * LANES)
            lines[e, 0, :, span] = column(0, 0) + v * (column(0, 1) + v * (column(0, 2) + v * column(0, 3)))
            lines[e, 1, :, span] = column(1, 0) + v * (column(1, 1) + v * column(1, 2))
            lines[e, 2, :, span] = column(2, 0) + v * column(2, 1)
            lines[e, 3, :, span] = column(3, 0)


def weighted_sums(members, lines, rows, col_band, size, u):
    totals = [None] * len(members)
    for b in range(col_band.shape[0]):
        window = jnp.concatenate(
            [rows[e, b * size : (b + 1) * size, s * LANES : (s + 1) * LANES] for e, s in members], axis=0
        )
        along = jnp.dot(window, col_band[b], preferred_element_type=F32)
        for i, (e, s) in enumerate(members):
            r0, r1, r2, r3 = (lines[e, p, b : b + 1, s * LANES : (s + 1) * LANES] for p in range(4))
            value = (r0 + u * (r1 + u * (r2 + u * r3))) * along[i * size : (i + 1) * size]
            totals[i] = value if b == 0 else totals[i] + value
    return totals


def joined(blocks, parts, width):
    out = []
    for low in range(0, width, LANES):
        lane = low + lax.broadcasted_iota(jnp.int32, blocks[0].shape, 1)
        tile = None
        for block, (at, size) in zip(blocks, parts):
            if at < low + LANES and at + size > low:
                tile = block if tile is None else jnp.where(lane >= at, block, tile)
        out.append(tile)
    return jnp.concatenate(out, axis=1)


def row_position(first, rows, total_rows):
    row_at = first + lax.broadcasted_iota(jnp.int32, (rows, LANES), 0)
    return (2.0 * row_at.astype(F32) + 1.0) / total_rows - 1.0


def inner_kernel(k, shares, total_rows, half, warped, active, covered, inner_band, col_band, matched, strip, rows, lines):
    exp_count, row_count, col_count = warped.shape
    basis_count, size, _ = inner_band.shape
    _, inner, width = matched.shape
    parts = segments(width, 2 * half + 1)
    start = share_start(k, shares, width)
    u = row_position(lax.axis_index("sky") * row_count + EDGE, size, total_rows)
    line_polynomials(active, lines, start, parts, col_count)
    band = inner_band[...].reshape(basis_count * size, LANES)
    for e in range(exp_count):

        def read(at, count):
            own = warped[e, :, pl.ds(at, count)].astype(F32)
            return jnp.concatenate([own, jnp.zeros((LANES - row_count, count), F32)], axis=0)

        strip[e] = windows_of(read, start, width, col_count, parts, half)
        rows[e] = jnp.dot(band, strip[e], preferred_element_type=F32).astype(BF16)
    for e in range(exp_count):
        blocks = []
        for first in range(0, len(parts), GROUP):
            members = [(e, s) for s in range(first, min(first + GROUP, len(parts)))]
            blocks += weighted_sums(members, lines, rows, col_band, size, u)
        counts = jnp.concatenate([covered[e, EDGE : EDGE + inner]] * (width // LANES), axis=1) > 0
        matched[e] = jnp.where(counts, joined(blocks, parts, width)[:inner], jnp.inf).astype(BF16)


def outer_kernel(shares, total_rows, half, warped, near, far, active, covered, outer_band, col_band, *refs):
    matched, (strip, rows, lines) = refs[:shares], refs[shares:]
    exp_count, row_count, col_count = warped.shape
    basis_count, size, _ = outer_band.shape
    width = matched[0].shape[2]
    parts = segments(width, 2 * half + 1)
    span = LANES // 2 - EDGE
    sky = lax.axis_index("sky")
    even = lax.rem(sky, 2) == 0
    u = jnp.concatenate(
        [
            row_position(sky * row_count, EDGE, total_rows),
            row_position((sky + 1) * row_count - EDGE, EDGE, total_rows),
        ],
        axis=0,
    )
    band = outer_band[...].reshape(basis_count * size, LANES)
    for k in range(shares):
        start = share_start(k, shares, width)
        line_polynomials(active, lines.at[k], start, parts, col_count)
        for e in range(exp_count):

            def read(at, count):
                own = warped[e, :, pl.ds(at, count)].astype(F32)
                same = near[e, :, pl.ds(at, count)].astype(F32)
                other = far[e, :, pl.ds(at, count)].astype(F32)
                up, down = jnp.where(even, other, same), jnp.where(even, same, other)
                return jnp.concatenate([up, own[:span], own[row_count - span :], down], axis=0)

            strip[k, e] = windows_of(read, start, width, col_count, parts, half)
            rows[k, e] = jnp.dot(band, strip[k, e], preferred_element_type=F32).astype(BF16)
    for k in range(shares):
        members = [(e, s) for e in range(exp_count) for s in range(len(parts))]
        blocks = weighted_sums(members, lines.at[k], rows.at[k], col_band, size, u)
        for e in range(exp_count):
            own = blocks[e * len(parts) : (e + 1) * len(parts)]
            counts = jnp.concatenate([covered[e, :EDGE], covered[e, row_count - EDGE :]], axis=0)
            counts = jnp.concatenate([counts] * (width // LANES), axis=1) > 0
            matched[k][e] = jnp.where(counts, joined(own, parts, width), jnp.inf).astype(BF16)


def coadd_kernel(shares, *refs):
    inner, outer, variances, coadd = refs[:shares], refs[shares : 2 * shares], refs[2 * shares : 3 * shares], refs[-1]
    exp_count, row_count, width = variances[0].shape
    for j in range(width // LANES):
        span = slice(j * LANES, (j + 1) * LANES)
        values, spreads, weights = [], [], []
        for k in range(shares):
            for e in range(exp_count):
                edges = outer[k][e, :, span].astype(F32)
                value = jnp.concatenate([edges[:EDGE], inner[k][e, :, span].astype(F32), edges[EDGE:]], axis=0)
                counts = value < jnp.inf
                spread = jnp.where(counts, variances[k][e, :, span].astype(F32), jnp.inf)
                values.append(jnp.where(counts, value, 0.0))
                spreads.append(spread)
                weights.append(1.0 / spread)
        first = sum(w * x for w, x in zip(weights, values)) / (1.0 + sum(weights))
        robust = [1.0 / (s + (x - first) * (x - first) * (1.0 / 9.0)) for s, x in zip(spreads, values)]
        coadd[:, span] = sum(r * x for r, x in zip(robust, values)) / (1.0 + sum(robust))


def body(warped, variance, basis_taps, coeffs, degrees, footprint, masks):
    exp_count, row_count, col_count = warped.shape
    basis_count, _, tap_count = basis_taps.shape
    half = tap_count // 2
    sky_count, shares = lax.axis_size("sky"), lax.axis_size("exp")
    width = col_count // shares
    total_rows = row_count * sky_count
    inner = row_count - 2 * EDGE
    size = round_up(inner, 16)
    spans = len(segments(width, tap_count)) * LANES
    vmem = pl.BlockSpec(memory_space=pltpu.VMEM)

    def array(*shape, dtype=BF16):
        return jax.ShapeDtypeStruct(shape, dtype)

    def call(kernel, name, out_shape, *operands, scratch=(), mebibytes=8, cost=0.1):
        outputs = len(out_shape) if isinstance(out_shape, list) else 0
        return pl.pallas_call(
            kernel,
            out_shape=out_shape,
            in_specs=[vmem] * len(operands),
            out_specs=[vmem] * outputs if outputs else vmem,
            scratch_shapes=scratch,
            compiler_params=pltpu.CompilerParams(vmem_limit_bytes=mebibytes * 2**20),
            cost_estimate=pl.CostEstimate(flops=int(cost * 1e9), bytes_accessed=int(cost * 3e6), transcendentals=0),
            name=name,
        )(*operands)

    def to_share(values, k):
        return lax.ppermute(values, "exp", [(i, (i + k) % shares) for i in range(shares)])

    variances = call(variance_kernel, "variance", [array(exp_count, row_count, width)] * shares, variance)
    variances = [variances[0]] + [to_share(variances[k], k) for k in range(1, shares)]

    edge = array(exp_count, EDGE, col_count)
    near, far = call(edges_kernel, "edges", [edge, edge], warped)
    near = lax.ppermute(near, "sky", [(i, i ^ 1) for i in range(sky_count) if i ^ 1 < sky_count])
    pairs = [(i, i + 1) for i in range(1, sky_count - 1, 2)]
    far = lax.ppermute(far, "sky", pairs + [(j, i) for i, j in pairs])

    inner_band, outer_band, col_band, active, covered = call(
        setup_kernel,
        "setup",
        [
            array(basis_count, size, LANES),
            array(basis_count, 2 * EDGE, LANES),
            array(basis_count, LANES, LANES),
            array(exp_count, 16, LANES, dtype=F32),
            array(exp_count, row_count, LANES, dtype=F32),
        ],
        basis_taps,
        jnp.transpose(coeffs, (1, 0, 2)),
        degrees,
        footprint,
        masks,
        cost=0.6,
    )

    def inside(k):
        return call(
            functools.partial(inner_kernel, k, shares, total_rows, half),
            "inner",
            array(exp_count, inner, width),
            warped,
            active,
            covered,
            inner_band,
            col_band,
            scratch=[
                pltpu.VMEM((exp_count, LANES, spans), BF16),
                pltpu.VMEM((exp_count, basis_count * size, spans), BF16),
                pltpu.VMEM((exp_count, 4, 16, spans), F32),
            ],
            mebibytes=12,
            cost=2.0,
        )

    inners = [None] + [to_share(inside(k), k) for k in range(1, shares)]
    variances, near = lax.optimization_barrier((variances, near))
    outers = call(
        functools.partial(outer_kernel, shares, total_rows, half),
        "outer",
        [array(exp_count, 2 * EDGE, width)] * shares,
        warped,
        near,
        far,
        active,
        covered,
        outer_band,
        col_band,
        scratch=[
            pltpu.VMEM((shares, exp_count, LANES, spans), BF16),
            pltpu.VMEM((shares, exp_count, basis_count * 2 * EDGE, spans), BF16),
            pltpu.VMEM((shares, exp_count, 4, 16, spans), F32),
        ],
        mebibytes=12,
        cost=1.5,
    )
    outers = [outers[0]] + [to_share(outers[k], k) for k in range(1, shares)]
    inners[0] = inside(0)

    return call(
        functools.partial(coadd_kernel, shares),
        "coadd",
        array(row_count, width, dtype=F32),
        *inners,
        *outers,
        *variances,
        cost=0.5,
    )


def solution(mesh):
    in_specs = (
        P("exp", "sky", None),
        P("exp", "sky", None),
        P(),
        P("exp", None, None),
        P("exp", None),
        P("exp", None),
        P("exp", "sky"),
    )
    return jax.shard_map(body, mesh=mesh, in_specs=in_specs, out_specs=P("sky", "exp"), check_vma=False)
```

time: 31.7 us -> 19.1 us (0.60)
  the two profiles are of different devices: /device:TPU:23 before, /device:TPU:5 now
where the time goes in v2:
time: 19.1 us; the launch traced here: 18.9 us
  Pallas kernels  8.8 us (46%)
  starting transfers between devices  6.95 us (36%)
  waiting for transfers between devices  2.04 us (11%)
  local copies, waits for them, and re-layouts  1.06 us (6%)
    pallas_call x7, Pallas kernels, call(): pl.pallas_call(kernel, out_shape=out_shape, in_specs=[vmem] * len(operand...  8.8 us
    ppermute x1, starting transfers between devices, body(): far = lax.ppermute(far, 'sky', pairs + [(j, i) for i, j in pairs])  3.06 us
    ppermute x3, starting transfers between devices, to_share(): lax.ppermute(values, 'exp', [(i, (i + k) % shares) for i in range(shares)])  2.88 us
    ppermute x3, waiting for transfers between devices, to_share(): lax.ppermute(values, 'exp', [(i, (i + k) % shares) for i in range(shares)])  2.03 us
    unnamed x14, local copies, waits for them, and re-layouts  1.06 us
    ppermute x1, starting transfers between devices, body(): lax.ppermute(near, 'sky', [(i, i ^ 1) for i in range(sky_count) if i ^ 1...  1.02 us
  transfers between devices with their start and end apart: 5, of which 2 were waited for; matrix products, arithmetic and copies ran while one was open for 0% of the time, Pallas kernels for 40%

profile of v2, /device:TPU:5, one launch (start us, length us, event | category | flops | bytes accessed | tf_op | source)
XLA Modules:
  0.0 18.9 jit_solution(3133051668621428106)
XLA Ops:
  0.0 0.0 copy-start
  0.0 1.0 %copy-done = bf16[2,120,1024]{2,1,0:T(8,128)(2,1)S(1)} copy-done((bf16[2,120,1024]{2,1,0:T(8,128)(2,1)S(1)}, bf16[2,120,1024]{2,1,0:T(8,128)(2,1)}, u32[]{:S(2)}) %copy-start) | copy-done | bytes 491544
  1.0 0.0 copy-start.1
  1.1 0.0 copy-start.2
  1.1 1.3 %collective-permute-start.1 = (bf16[2,120,512]{2,1,0:T(8,128)(2,1)S(1)}, bf16[2,120,512]{2,1,0:T(8,128)(2,1)S(1)}, u32[]{:S(2)}, u32[]{:S(2)}) collective-permute-start(bf16[2,120,512]{2,1,0:T(8,128)(2,1)S(1)} %get-tuple-element.24), channel_id=1, source_target_pairs={{0,1},{1,0},{2,3},{3,2},{4,5},{5,4},{6,7},{7,6},{8,9},{9,8},{10,11... | collective-permute-start | bytes 737288 | tf_op jit(solution)/shard_map/ppermute | solution.py:284
  2.4 0.0 copy-done.1
  2.4 0.0 copy-start.5
  2.4 0.0 copy-start.6
  2.4 0.0 copy-start.3
  2.4 1.0 %collective-permute-start.2 = (bf16[2,16,1024]{2,1,0:T(8,128)(2,1)S(1)}, bf16[2,16,1024]{2,1,0:T(8,128)(2,1)S(1)}, u32[]{:S(2)}, u32[]{:S(2)}) collective-permute-start(bf16[2,16,1024]{2,1,0:T(8,128)(2,1)S(1)} %get-tuple-element.25), channel_id=1, source_target_pairs={{0,2},{2,0},{4,6},{6,4},{8,10},{10,8},{12,14},{14,12},{16,18},{18,... | collective-permute-start | bytes 196616 | tf_op jit(solution)/shard_map/ppermute | solution.py:291
  3.4 0.0 copy-start.4
  3.4 3.1 %collective-permute-start.3 = (bf16[2,16,1024]{2,1,0:T(8,128)(2,1)S(1)}, bf16[2,16,1024]{2,1,0:T(8,128)(2,1)S(1)}, u32[]{:S(2)}, u32[]{:S(2)}) collective-permute-start(bf16[2,16,1024]{2,1,0:T(8,128)(2,1)S(1)} %get-tuple-element.27), channel_id=1, source_target_pairs={{2,4},{6,8},{10,12},{14,16},{18,20},{22,24},{26,28},{4,2},{8,6},{1... | collective-permute-start | bytes 196616 | tf_op jit(solution)/shard_map/ppermute | solution.py:293
  6.5 0.0 copy-done.2
  6.5 0.0 copy-done.5
  6.5 0.0 copy-done.6
  6.5 0.0 copy-done.3
  6.5 0.0 copy-done.4
  6.6 0.5 %setup.1 = (bf16[9,96,128]{2,1,0:T(8,128)(2,1)S(1)}, bf16[9,32,128]{2,1,0:T(8,128)(2,1)S(1)}, bf16[9,128,128]{2,1,0:T(8,128)(2,1)S(1)}, f32[2,16,128]{2,1,0:T(8,128)S(1)}, f32[2,120,128]{2,1,0:T(8,128)S(1)}) custom-call(bf16[9,2,23]{2,1,0:T(2,128)(2,1)S(1)} %copy-done.3, f32[9,2,10]{2,1,0:T(2,128)S(1)} %bitcast.1, s32[2,9]{1,0:T(2,128)S(1)} %copy-done.4, ...), custom_call_target="tpu_custom_call" | custom-call | flops 600000000 | bytes 1800000 | tf_op jit(solution)/shard_map/setup/pallas_call | solution.py:272
  7.0 2.6 %inner.3 = bf16[2,88,512]{2,1,0:T(8,128)(2,1)S(1)} custom-call(bf16[2,120,1024]{2,1,0:T(8,128)(2,1)S(1)} %copy-done.1, f32[2,16,128]{2,1,0:T(8,128)S(1)} %get-tuple-element.19.active, f32[2,120,128]{2,1,0:T(8,128)S(1)} %get-tuple-element.20.covered, bf16[9,96,128]{2,1,0:T(8,128)(2,1)S(1)} %get-tuple-element.21.inner_band, ...), custom_call_target="tpu_custom_call" | custom-call | flops 2000000000 | bytes 6000000 | tf_op jit(solution)/shard_map/inner/pallas_call | solution.py:272
  9.7 0.6 %collective-permute-start = (bf16[2,88,512]{2,1,0:T(8,128)(2,1)S(1)}, bf16[2,88,512]{2,1,0:T(8,128)(2,1)S(1)}, u32[]{:S(2)}, u32[]{:S(2)}) collective-permute-start(bf16[2,88,512]{2,1,0:T(8,128)(2,1)S(1)} %inner.3), channel_id=1, source_target_pairs={{0,1},{1,0},{2,3},{3,2},{4,5},{5,4},{6,7},{7,6},{8,9},{9,8},{10,11... | collective-permute-start | bytes 540680 | tf_op jit(solution)/shard_map/ppermute | solution.py:284
  10.3 0.0 collective-permute-done.2.near
  10.3 0.0 collective-permute-done.1.refs_5_
  10.3 0.0 collective-permute-done.3.far
  10.3 1.8 %outer.1 = (bf16[2,32,512]{2,1,0:T(8,128)(2,1)S(1)}, bf16[2,32,512]{2,1,0:T(8,128)(2,1)S(1)}) custom-call(bf16[2,120,1024]{2,1,0:T(8,128)(2,1)S(1)} %copy-done.1, bf16[2,16,1024]{2,1,0:T(8,128)(2,1)S(1)} %collective-permute-done.2.near, bf16[2,16,1024]{2,1,0:T(8,128)(2,1)S(1)} %collective-permute-done.3.far, f32[2,16,128]{2,1,0:T(8,128)S(1)} %get-tuple-element.19.active, ...), custom_call_target="tpu_custom_call" | custom-call | flops 1500000000 | bytes 4500000 | tf_op jit(solution)/shard_map/outer/pallas_call | solution.py:272
  12.1 1.0 %collective-permute-start.4 = (bf16[2,32,512]{2,1,0:T(8,128)(2,1)S(1)}, bf16[2,32,512]{2,1,0:T(8,128)(2,1)S(1)}, u32[]{:S(2)}, u32[]{:S(2)}) collective-permute-start(bf16[2,32,512]{2,1,0:T(8,128)(2,1)S(1)} %get-tuple-element.30), channel_id=1, source_target_pairs={{0,1},{1,0},{2,3},{3,2},{4,5},{5,4},{6,7},{7,6},{8,9},{9,8},{10,11... | collective-permute-start | bytes 196616 | tf_op jit(solution)/shard_map/ppermute | solution.py:284
  13.1 2.6 %inner.2.refs_0_ = bf16[2,88,512]{2,1,0:T(8,128)(2,1)S(1)} custom-call(bf16[2,120,1024]{2,1,0:T(8,128)(2,1)S(1)} %copy-done.1, f32[2,16,128]{2,1,0:T(8,128)S(1)} %get-tuple-element.19.active, f32[2,120,128]{2,1,0:T(8,128)S(1)} %get-tuple-element.20.covered, bf16[9,96,128]{2,1,0:T(8,128)(2,1)S(1)} %get-tuple-element.21.inner_band, ...), custom_call_target="tpu_custom_call" | custom-call | flops 2000000000 | bytes 6000000 | tf_op jit(solution)/shard_map/inner/pallas_call | solution.py:272
  15.6 0.6 %collective-permute-done.refs_1_ = bf16[2,88,512]{2,1,0:T(8,128)(2,1)S(1)} collective-permute-done((bf16[2,88,512]{2,1,0:T(8,128)(2,1)S(1)}, bf16[2,88,512]{2,1,0:T(8,128)(2,1)S(1)}, u32[]{:S(2)}, u32[]{:S(2)}) %collective-permute-start) | collective-permute-done | bytes 180256 | tf_op jit(solution)/shard_map/ppermute | solution.py:284
  16.3 1.4 %collective-permute-done.4.refs_3_ = bf16[2,32,512]{2,1,0:T(8,128)(2,1)S(1)} collective-permute-done((bf16[2,32,512]{2,1,0:T(8,128)(2,1)S(1)}, bf16[2,32,512]{2,1,0:T(8,128)(2,1)S(1)}, u32[]{:S(2)}, u32[]{:S(2)}) %collective-permute-start.4) | collective-permute-done | bytes 65568 | tf_op jit(solution)/shard_map/ppermute | solution.py:284
  17.7 1.3 %coadd.1 = f32[120,512]{1,0:T(8,128)} custom-call(bf16[2,88,512]{2,1,0:T(8,128)(2,1)S(1)} %inner.2.refs_0_, bf16[2,88,512]{2,1,0:T(8,128)(2,1)S(1)} %collective-permute-done.refs_1_, bf16[2,32,512]{2,1,0:T(8,128)(2,1)S(1)} %get-tuple-element.29.refs_2_, bf16[2,32,512]{2,1,0:T(8,128)(2,1)S(1)} %collective-permute-done.4.refs_3_, ...), custom_call_target="tpu_custom_call" | custom-call | flops 500000000 | bytes 1500000 | tf_op jit(solution)/shard_map/coadd/pallas_call | solution.py:272
  (2 shorter events, 0.1 us)
Async XLA Ops:
  0.0 1.0 %copy-start = (bf16[2,120,1024]{2,1,0:T(8,128)(2,1)S(1)}, bf16[2,120,1024]{2,1,0:T(8,128)(2,1)}, u32[]{:S(2)}) copy-start(bf16[2,120,1024]{2,1,0:T(8,128)(2,1)} %variance.3) | copy-start | bytes 1474564
  1.0 1.3 %copy-start.1 = (bf16[2,120,1024]{2,1,0:T(8,128)(2,1)S(1)}, bf16[2,120,1024]{2,1,0:T(8,128)(2,1)}, u32[]{:S(2)}) copy-start(bf16[2,120,1024]{2,1,0:T(8,128)(2,1)} %warped.7) | copy-start | bytes 1474564
  1.1 5.4 %copy-start.2 = (f32[2,9,10]{2,0,1:T(2,128)S(1)}, f32[2,9,10]{2,0,1:T(2,128)}, u32[]{:S(2)}) copy-start(f32[2,9,10]{2,0,1:T(2,128)} %param.10) | copy-start | bytes 2164
  1.1 9.2 %collective-permute-start.1 = (bf16[2,120,512]{2,1,0:T(8,128)(2,1)S(1)}, bf16[2,120,512]{2,1,0:T(8,128)(2,1)S(1)}, u32[]{:S(2)}, u32[]{:S(2)}) collective-permute-start(bf16[2,120,512]{2,1,0:T(8,128)(2,1)S(1)} %get-tuple-element.24), channel_id=1, source_target_pairs={{0,1},{1,0},{2,3},{3,2},{4,5},{5,4},{6,7},{7,6},{8,9},{9,8},{10,11... | collective-permute-start | bytes 737288 | tf_op jit(solution)/shard_map/ppermute | solution.py:284
  2.4 4.2 %copy-start.5 = (s32[2,2]{1,0:T(2,128)S(1)}, s32[2,2]{1,0:T(2,128)}, u32[]{:S(2)}) copy-start(s32[2,2]{1,0:T(2,128)} %footprint.1) | copy-start | bytes 52
  2.4 4.2 %copy-start.6 = (s32[2,8]{1,0:T(2,128)S(1)}, s32[2,8]{1,0:T(2,128)}, u32[]{:S(2)}) copy-start(s32[2,8]{1,0:T(2,128)} %masks.1) | copy-start | bytes 196
  2.4 4.1 %copy-start.3 = (bf16[9,2,23]{2,1,0:T(2,128)(2,1)S(1)}, bf16[9,2,23]{2,1,0:T(2,128)(2,1)}, u32[]{:S(2)}) copy-start(bf16[9,2,23]{2,1,0:T(2,128)(2,1)} %taps.1) | copy-start | bytes 2488
  2.4 7.9 %collective-permute-start.2 = (bf16[2,16,1024]{2,1,0:T(8,128)(2,1)S(1)}, bf16[2,16,1024]{2,1,0:T(8,128)(2,1)S(1)}, u32[]{:S(2)}, u32[]{:S(2)}) collective-permute-start(bf16[2,16,1024]{2,1,0:T(8,128)(2,1)S(1)} %get-tuple-element.25), channel_id=1, source_target_pairs={{0,2},{2,0},{4,6},{6,4},{8,10},{10,8},{12,14},{14,12},{16,18},{18,... | collective-permute-start | bytes 196616 | tf_op jit(solution)/shard_map/ppermute | solution.py:291
  3.4 3.1 %copy-start.4 = (s32[2,9]{1,0:T(2,128)S(1)}, s32[2,9]{1,0:T(2,128)}, u32[]{:S(2)}) copy-start(s32[2,9]{1,0:T(2,128)} %degrees.1) | copy-start | bytes 220
  3.4 6.9 %collective-permute-start.3 = (bf16[2,16,1024]{2,1,0:T(8,128)(2,1)S(1)}, bf16[2,16,1024]{2,1,0:T(8,128)(2,1)S(1)}, u32[]{:S(2)}, u32[]{:S(2)}) collective-permute-start(bf16[2,16,1024]{2,1,0:T(8,128)(2,1)S(1)} %get-tuple-element.27), channel_id=1, source_target_pairs={{2,4},{6,8},{10,12},{14,16},{18,20},{22,24},{26,28},{4,2},{8,6},{1... | collective-permute-start | bytes 196616 | tf_op jit(solution)/shard_map/ppermute | solution.py:293
  9.7 6.6 %collective-permute-start = (bf16[2,88,512]{2,1,0:T(8,128)(2,1)S(1)}, bf16[2,88,512]{2,1,0:T(8,128)(2,1)S(1)}, u32[]{:S(2)}, u32[]{:S(2)}) collective-permute-start(bf16[2,88,512]{2,1,0:T(8,128)(2,1)S(1)} %inner.3), channel_id=1, source_target_pairs={{0,1},{1,0},{2,3},{3,2},{4,5},{5,4},{6,7},{7,6},{8,9},{9,8},{10,11... | collective-permute-start | bytes 540680 | tf_op jit(solution)/shard_map/ppermute | solution.py:284
  12.1 5.5 %collective-permute-start.4 = (bf16[2,32,512]{2,1,0:T(8,128)(2,1)S(1)}, bf16[2,32,512]{2,1,0:T(8,128)(2,1)S(1)}, u32[]{:S(2)}, u32[]{:S(2)}) collective-permute-start(bf16[2,32,512]{2,1,0:T(8,128)(2,1)S(1)} %get-tuple-element.30), channel_id=1, source_target_pairs={{0,1},{1,0},{2,3},{3,2},{4,5},{5,4},{6,7},{7,6},{8,9},{9,8},{10,11... | collective-permute-start | bytes 196616 | tf_op jit(solution)/shard_map/ppermute | solution.py:284

commit v3 on v2

v3 whole, which is shorter than its diff:
```python
import functools

import jax
import jax.numpy as jnp
from jax import lax
from jax.experimental import pallas as pl
from jax.experimental.pallas import tpu as pltpu
from jax.sharding import PartitionSpec as P

POWERS = ((0, 0), (1, 0), (0, 1), (2, 0), (1, 1), (0, 2), (3, 0), (2, 1), (1, 2), (0, 3))
TERM = {power: index for index, power in enumerate(POWERS)}
ROWS_PER_WORD = 15
EDGE = 16
LANES = 128
GROUP = 3
PIECES = 6
F32 = jnp.float32
BF16 = jnp.bfloat16


def round_up(value, unit):
    return -(-value // unit) * unit


def segments(width, tap_count):
    valid = LANES - tap_count + 1
    return [(at, min(valid, width - at)) for at in range(0, width, valid)]


def share_start(k, shares, width):
    return pl.multiple_of(lax.rem(lax.axis_index("exp") + k, shares) * width, LANES)


def variance_kernel(variance, *parts):
    shares, width = len(parts), parts[0].shape[2]
    for k in range(shares):
        parts[k][...] = variance[:, :, pl.ds(share_start(k, shares, width), width)]


def edges_kernel(warped, near, far):
    row_count = warped.shape[1]
    even = lax.rem(lax.axis_index("sky"), 2) == 0
    for e in range(warped.shape[0]):
        image = warped[e].astype(F32)
        head, tail = image[:EDGE], image[row_count - EDGE :]
        near[e] = jnp.where(even, tail, head).astype(BF16)
        far[e] = jnp.where(even, head, tail).astype(BF16)


def pieces(value):
    high = value.astype(BF16).astype(F32)
    rest = value - high
    middle = rest.astype(BF16).astype(F32)
    return high, middle, rest - middle


def row_features(first, size, total_rows):
    u = row_position(first, size, total_rows)
    lane = lax.broadcasted_iota(jnp.int32, u.shape, 1)
    power, group = (lane >> 1) & 3, lane >> 3
    value = jnp.where(power == 0, 1.0, jnp.where(power == 1, u, jnp.where(power == 2, u * u, u * u * u)))
    high, middle, low = pieces(value)
    value = jnp.where((group == 1) | (group == 4), middle, jnp.where(group == 2, low, high))
    value = jnp.where(group < PIECES, value, 0.0)
    odd = (lane & 1) == 1
    return jnp.where(odd, 0.0, value).astype(BF16), jnp.where(odd, value, 0.0).astype(BF16)


def setup_kernel(
    total_rows, taps, coeffs, degrees, footprint, masks,
    inner_band, outer_band, col_band, active, covered, inner_features, outer_features
):
    basis_count, _, tap_count = taps.shape
    exp_count, row_count, _ = covered.shape
    half = tap_count // 2
    inner = inner_band.shape[1]

    both = jnp.concatenate([taps[b].astype(F32) for b in range(basis_count)], axis=0)
    lines = jnp.concatenate([both, jnp.zeros((2 * basis_count, LANES - tap_count), F32)], axis=1).astype(BF16)
    lane = lax.broadcasted_iota(jnp.int32, (LANES, LANES), 1)
    tap = lax.broadcasted_iota(jnp.int32, (LANES, LANES), 0)
    flip = (lane + tap == LANES).astype(F32) + ((lane == 0) & (tap == 0)).astype(F32)
    flipped = jnp.dot(lines, flip.astype(BF16), preferred_element_type=F32)
    lines = lines.astype(F32)

    def circulant(line, size):
        return pltpu.roll(jnp.broadcast_to(line, (size, LANES)), 0, 1, stride=1, stride_axis=0)

    near = pltpu.roll(lines, EDGE - half, 1)
    far = pltpu.roll(lines, LANES - 2 * EDGE - half, 1)
    for b in range(basis_count):
        upper = circulant(near[2 * b : 2 * b + 1], inner)
        lower = circulant(far[2 * b : 2 * b + 1], EDGE)
        inner_band[b] = upper.astype(BF16)
        outer_band[b] = jnp.concatenate([upper[:EDGE], lower], axis=0).astype(BF16)
        col_band[b] = circulant(flipped[2 * b + 1 : 2 * b + 2], LANES).astype(BF16)

    term_count = coeffs.shape[2]
    term = lax.broadcasted_iota(jnp.int32, (1, term_count), 1)
    order = jnp.zeros((1, term_count), F32)
    for index, (p, q) in enumerate(POWERS):
        order = jnp.where(term == index, float(p + q), order)
    wide = jnp.concatenate([degrees[...].astype(F32), jnp.zeros((exp_count, LANES - basis_count), F32)], axis=1)
    by_basis = jnp.concatenate([wide, jnp.zeros((8 - exp_count, LANES), F32)], axis=0).T
    local = lax.broadcasted_iota(jnp.int32, (row_count, LANES), 0)
    total = local + lax.axis_index("sky") * row_count
    for e in range(exp_count):
        own = jnp.concatenate([coeffs[b, e : e + 1, :] for b in range(basis_count)], axis=0)
        kept = jnp.where(order <= by_basis[:basis_count, e : e + 1], own, 0.0)
        kept = jnp.concatenate([kept, jnp.zeros((16 - basis_count, term_count), F32)], axis=0)
        kept = jnp.concatenate([kept, jnp.zeros((16, LANES - term_count), F32)], axis=1)
        place = lax.broadcasted_iota(jnp.int32, kept.shape, 1)
        powers = []
        for p in range(4):
            value = jnp.zeros_like(kept)
            for q in range(4 - p):
                value = jnp.where(place == q, pltpu.roll(kept, (q - TERM[p, q]) % LANES, 1), value)
            powers.append(value)
        for pair in range(active.shape[1]):
            active[e, pair] = jnp.concatenate([value[2 * pair : 2 * pair + 2] for value in powers], axis=0)
        word = jnp.broadcast_to(masks[e : e + 1, 0:1], (row_count, LANES))
        first = jnp.zeros((row_count, LANES), jnp.int32)
        for w in range(1, masks.shape[1]):
            here = local >= w * ROWS_PER_WORD
            word = jnp.where(here, jnp.broadcast_to(masks[e : e + 1, w : w + 1], (row_count, LANES)), word)
            first = jnp.where(here, w * ROWS_PER_WORD, first)
        planes = lax.shift_right_logical(word, 2 * (local - first)) & 3
        low = jnp.broadcast_to(footprint[e : e + 1, 0:1], (row_count, LANES))
        high = jnp.broadcast_to(footprint[e : e + 1, 1:2], (row_count, LANES))
        covered[e] = ((total >= low) & (total < high) & (planes != 3)).astype(F32)
    top = lax.axis_index("sky") * row_count
    for odd, value in enumerate(row_features(top + EDGE, inner, total_rows)):
        inner_features[odd * inner : (odd + 1) * inner] = value
    upper = row_features(top, EDGE, total_rows)
    lower = row_features(top + row_count - EDGE, EDGE, total_rows)
    for odd in range(2):
        outer_features[2 * EDGE * odd : 2 * EDGE * (odd + 1)] = jnp.concatenate([upper[odd], lower[odd]], axis=0)


def windows_of(read, start, width, col_count, parts, half):
    left_at = pl.multiple_of(jnp.maximum(start - LANES, 0), LANES)
    right_at = pl.multiple_of(jnp.minimum(start + width, col_count - LANES), LANES)
    left = jnp.where(start > 0, read(left_at, LANES), 0.0)
    right = jnp.where(start + width < col_count, read(right_at, LANES), 0.0)
    middle = read(start, width)
    blocks = [left] + [middle[:, at : at + LANES] for at in range(0, width, LANES)] + [right]
    blocks = [pltpu.roll(block, half, 1) for block in blocks]
    lane = lax.broadcasted_iota(jnp.int32, left.shape, 1)
    place = jnp.where(lane >= half, lane - half, lane - half + LANES)
    pieces = []
    for at, _ in parts:
        base, offset = divmod(LANES + at - half, LANES)
        pieces.append(jnp.where(place >= offset, blocks[base], blocks[base + 1]))
    return jnp.concatenate(pieces, axis=1).astype(BF16)


def line_polynomials(active, lines, start, parts, col_count):
    exp_count, pair_count, rows, _ = active.shape
    lane = lax.broadcasted_iota(jnp.int32, (rows, LANES), 1)
    for s, (at, _) in enumerate(parts):
        col_at = at + jnp.where(lane >= at % LANES, lane - at % LANES, lane - at % LANES + LANES)
        v = (2.0 * (start + col_at).astype(F32) + 1.0) / col_count - 1.0
        span = slice(s * LANES, (s + 1) * LANES)
        for e in range(exp_count):
            for pair in range(pair_count):
                values = active[e, pair]
                c0, c1, c2, c3 = (jnp.broadcast_to(values[:, q : q + 1], values.shape) for q in range(4))
                high, middle, low = pieces(c0 + v * (c1 + v * (c2 + v * c3)))
                lines[e, pair, 0:16, span] = jnp.concatenate([high, high], axis=0).astype(BF16)
                lines[e, pair, 16:32, span] = jnp.concatenate([high, middle], axis=0).astype(BF16)
                lines[e, pair, 32:48, span] = jnp.concatenate([middle, low], axis=0).astype(BF16)


def weighted_sums(e, parts, lines, features, rows, col_band, size):
    out = []
    for first in range(0, len(parts), GROUP):
        members = range(first, min(first + GROUP, len(parts)))
        span = slice(first * LANES, (members[-1] + 1) * LANES)
        totals = [None] * len(members)
        for b in range(col_band.shape[0]):
            odd = b % 2
            if not odd:
                field = jnp.dot(features[:, : 8 * PIECES], lines[e, b // 2, :, span], preferred_element_type=F32)
            window = jnp.concatenate(
                [rows[e, b * size : (b + 1) * size, s * LANES : (s + 1) * LANES] for s in members], axis=0
            )
            along = jnp.dot(window, col_band[b], preferred_element_type=F32)
            for i in range(len(members)):
                weight = field[odd * size : (odd + 1) * size, i * LANES : (i + 1) * LANES]
                value = weight * along[i * size : (i + 1) * size]
                totals[i] = value if b == 0 else totals[i] + value
        out += totals
    return out


def joined(blocks, parts, width):
    out = []
    for low in range(0, width, LANES):
        lane = low + lax.broadcasted_iota(jnp.int32, blocks[0].shape, 1)
        tile = None
        for block, (at, size) in zip(blocks, parts):
            if at < low + LANES and at + size > low:
                tile = block if tile is None else jnp.where(lane >= at, block, tile)
        out.append(tile)
    return jnp.concatenate(out, axis=1)


def row_position(first, rows, total_rows):
    row_at = first + lax.broadcasted_iota(jnp.int32, (rows, LANES), 0)
    return (2.0 * row_at.astype(F32) + 1.0) / total_rows - 1.0


def first_kernel(
    k, shares, half, warped, active, covered, features, inner_band, col_band, matched, lines, strip, rows
):
    exp_count, row_count, col_count = warped.shape
    basis_count, size, _ = inner_band.shape
    _, inner, width = matched.shape
    parts = segments(width, 2 * half + 1)
    start = share_start(k, shares, width)
    line_polynomials(active, lines, start, parts, col_count)
    band = inner_band[...].reshape(basis_count * size, LANES)
    for e in range(exp_count):

        def read(at, count):
            own = warped[e, :, pl.ds(at, count)].astype(F32)
            return jnp.concatenate([own, jnp.zeros((LANES - row_count, count), F32)], axis=0)

        strip[e] = windows_of(read, start, width, col_count, parts, half)
        rows[e] = jnp.dot(band, strip[e], preferred_element_type=F32).astype(BF16)
    for e in range(exp_count):
        blocks = weighted_sums(e, parts, lines, features, rows, col_band, size)
        counts = jnp.concatenate([covered[e, EDGE : EDGE + inner]] * (width // LANES), axis=1) > 0
        matched[e] = jnp.where(counts, joined(blocks, parts, width)[:inner], jnp.inf).astype(BF16)


def second_kernel(
    k, shares, half, warped, near, far, covered, features, outer_band, col_band, lines, matched, strip, rows
):
    exp_count, row_count, col_count = warped.shape
    basis_count, size, _ = outer_band.shape
    width = matched.shape[2]
    parts = segments(width, 2 * half + 1)
    span = LANES // 2 - EDGE
    sky = lax.axis_index("sky")
    even = lax.rem(sky, 2) == 0
    start = share_start(k, shares, width)
    band = outer_band[...].reshape(basis_count * size, LANES)
    for e in range(exp_count):

        def read(at, count):
            own = warped[e, :, pl.ds(at, count)].astype(F32)
            same = near[e, :, pl.ds(at, count)].astype(F32)
            other = far[e, :, pl.ds(at, count)].astype(F32)
            up, down = jnp.where(even, other, same), jnp.where(even, same, other)
            up = jnp.where(sky > 0, up, 0.0)
            down = jnp.where(sky < lax.axis_size("sky") - 1, down, 0.0)
            return jnp.concatenate([up, own[:span], own[row_count - span :], down], axis=0)

        strip[e] = windows_of(read, start, width, col_count, parts, half)
        rows[e] = jnp.dot(band, strip[e], preferred_element_type=F32).astype(BF16)
    for e in range(exp_count):
        blocks = weighted_sums(e, parts, lines, features, rows, col_band, size)
        counts = jnp.concatenate([covered[e, :EDGE], covered[e, row_count - EDGE :]], axis=0)
        counts = jnp.concatenate([counts] * (width // LANES), axis=1) > 0
        matched[e] = jnp.where(counts, joined(blocks, parts, width), jnp.inf).astype(BF16)


def robust_sum(fields, spreads):
    values, variances, weights = [], [], []
    for value, spread in zip(fields, spreads):
        counts = value < jnp.inf
        spread = jnp.where(counts, spread, jnp.inf)
        values.append(jnp.where(counts, value, 0.0))
        variances.append(spread)
        weights.append(1.0 / spread)
    first = sum(w * x for w, x in zip(weights, values)) / (1.0 + sum(weights))
    robust = [1.0 / (s + (x - first) * (x - first) * (1.0 / 9.0)) for s, x in zip(variances, values)]
    return sum(r * x for r, x in zip(robust, values)) / (1.0 + sum(robust))


def first_coadd_kernel(shares, *refs):
    fields, variances, coadd = refs[:shares], refs[shares : 2 * shares], refs[-1]
    exp_count, size, width = fields[0].shape
    pairs = [(k, e) for k in range(shares) for e in range(exp_count)]
    for at in range(0, width, LANES):
        span = slice(at, at + LANES)
        values = [fields[k][e, :, span].astype(F32) for k, e in pairs]
        spreads = [variances[k][e, :, span].astype(F32)[EDGE : EDGE + size] for k, e in pairs]
        coadd[:, span] = robust_sum(values, spreads)


def second_coadd_kernel(shares, *refs):
    fields, variances, done, coadd = refs[:shares], refs[shares : 2 * shares], refs[-2], refs[-1]
    exp_count, row_count, width = variances[0].shape
    size = done.shape[0]
    pairs = [(k, e) for k in range(shares) for e in range(exp_count)]
    coadd[EDGE : EDGE + size] = done[...]
    for at in range(0, width, LANES):
        span = slice(at, at + LANES)
        values = [fields[k][e, :, span].astype(F32) for k, e in pairs]
        spreads = []
        for k, e in pairs:
            spread = variances[k][e, :, span].astype(F32)
            spreads.append(jnp.concatenate([spread[:EDGE], spread[row_count - EDGE :]], axis=0))
        result = robust_sum(values, spreads)
        coadd[:EDGE, span] = result[:EDGE]
        coadd[row_count - EDGE :, span] = result[EDGE:]


def body(warped, variance, basis_taps, coeffs, degrees, footprint, masks):
    exp_count, row_count, col_count = warped.shape
    basis_count, _, tap_count = basis_taps.shape
    half = tap_count // 2
    sky_count, shares = lax.axis_size("sky"), lax.axis_size("exp")
    width = col_count // shares
    total_rows = row_count * sky_count
    inner = row_count - 2 * EDGE
    size = round_up(inner, 16)
    pair_count = -(-basis_count // 2)
    spans = len(segments(width, tap_count)) * LANES
    vmem = pl.BlockSpec(memory_space=pltpu.VMEM)

    def array(*shape, dtype=BF16):
        return jax.ShapeDtypeStruct(shape, dtype)

    def call(kernel, name, out_shape, *operands, scratch=(), mebibytes=8, cost=0.01):
        outputs = len(out_shape) if isinstance(out_shape, list) else 0
        return pl.pallas_call(
            kernel,
            out_shape=out_shape,
            in_specs=[vmem] * len(operands),
            out_specs=[vmem] * outputs if outputs else vmem,
            scratch_shapes=scratch,
            compiler_params=pltpu.CompilerParams(vmem_limit_bytes=mebibytes * 2**20),
            cost_estimate=pl.CostEstimate(flops=int(cost * 1e9), bytes_accessed=int(cost * 3e6), transcendentals=0),
            name=name,
        )(*operands)

    def to_share(values, k):
        return lax.ppermute(values, "exp", [(i, (i + k) % shares) for i in range(shares)])

    variances = call(variance_kernel, "variance", [array(exp_count, row_count, width)] * shares, variance)
    variances = [variances[0]] + [to_share(variances[k], k) for k in range(1, shares)]

    edge = array(exp_count, EDGE, col_count)
    near, far = call(edges_kernel, "edges", [edge, edge], warped)
    near = lax.ppermute(near, "sky", [(i, i ^ 1) for i in range(sky_count) if i ^ 1 < sky_count])
    partner = {i: i + 1 if i % 2 else i - 1 for i in range(1, sky_count)}
    pairs = []
    for i in range(sky_count):
        j = partner.get(i, i)
        ends = j in (i, sky_count)
        for e in range(shares):
            pairs.append((i * shares + e, i * shares + (e + 1) % shares if ends else j * shares + e))
    far = lax.ppermute(far, ("sky", "exp"), pairs)

    inner_band, outer_band, col_band, active, covered, inner_features, outer_features = call(
        functools.partial(setup_kernel, total_rows),
        "setup",
        [
            array(basis_count, size, LANES),
            array(basis_count, 2 * EDGE, LANES),
            array(basis_count, LANES, LANES),
            array(exp_count, pair_count, 8, LANES, dtype=F32),
            array(exp_count, row_count, LANES, dtype=F32),
            array(2 * size, LANES),
            array(4 * EDGE, LANES),
        ],
        basis_taps,
        jnp.transpose(coeffs, (1, 0, 2)),
        degrees,
        footprint,
        masks,
        cost=0.5,
    )

    def first(k):
        return call(
            functools.partial(first_kernel, k, shares, half),
            "first",
            [array(exp_count, inner, width), array(exp_count, pair_count, 8 * PIECES, spans)],
            warped,
            active,
            covered,
            inner_features,
            inner_band,
            col_band,
            scratch=[
                pltpu.VMEM((exp_count, LANES, spans), BF16),
                pltpu.VMEM((exp_count, basis_count * size, spans), BF16),
            ],
            mebibytes=12,
            cost=0.01 if k else 1.5,
        )

    def second(k, near, far, lines):
        return call(
            functools.partial(second_kernel, k, shares, half),
            "second",
            array(exp_count, 2 * EDGE, width),
            warped,
            near,
            far,
            covered,
            outer_features,
            outer_band,
            col_band,
            lines,
            scratch=[
                pltpu.VMEM((exp_count, LANES, spans), BF16),
                pltpu.VMEM((exp_count, basis_count * 2 * EDGE, spans), BF16),
            ],
            mebibytes=12,
            cost=0.01,
        )

    inner_features, near = lax.optimization_barrier((inner_features, near))
    firsts, seconds = [None] * shares, [None] * shares
    held = [None] * shares
    for k in range(1, shares):
        firsts[k], held[k] = first(k)
        firsts[k] = to_share(firsts[k], k)
    firsts[0], held[0] = first(0)
    variances, near, firsts[0] = lax.optimization_barrier((variances, near, firsts[0]))
    for k in range(1, shares):
        seconds[k] = second(k, near, far, held[k])
    seconds[1:], held[0] = lax.optimization_barrier((seconds[1:], held[0]))
    seconds[1:] = [to_share(seconds[k], k) for k in range(1, shares)]
    seconds[0] = second(0, near, far, held[0])

    done = call(
        functools.partial(first_coadd_kernel, shares),
        "first_coadd",
        array(inner, width, dtype=F32),
        *firsts,
        *variances,
        cost=0.01,
    )
    return call(
        functools.partial(second_coadd_kernel, shares),
        "second_coadd",
        array(row_count, width, dtype=F32),
        *seconds,
        *variances,
        done,
        cost=0.01,
    )


def solution(mesh):
    in_specs = (
        P("exp", "sky", None),
        P("exp", "sky", None),
        P(),
        P("exp", None, None),
        P("exp", None),
        P("exp", None),
        P("exp", "sky"),
    )
    return jax.shard_map(body, mesh=mesh, in_specs=in_specs, out_specs=P("sky", "exp"), check_vma=False)
```

time: 19.1 us -> 17.5 us (0.916)
  the two profiles are of different devices: /device:TPU:5 before, /device:TPU:0 now
where the time goes in v3:
time: 17.5 us; the launch traced here: 17.4 us
  Pallas kernels  7.86 us (45%)
  starting transfers between devices  6.79 us (39%)
  local copies, waits for them, and re-layouts  1.66 us (9%)
  waiting for transfers between devices  0.93 us (5%)
    pallas_call x9, Pallas kernels, call(): pl.pallas_call(kernel, out_shape=out_shape, in_specs=[vmem] * len(operand...  7.86 us
    ppermute x3, starting transfers between devices, to_share(): lax.ppermute(values, 'exp', [(i, (i + k) % shares) for i in range(shares)])  6.61 us
    unnamed x14, local copies, waits for them, and re-layouts  1.66 us
    ppermute x3, waiting for transfers between devices, to_share(): lax.ppermute(values, 'exp', [(i, (i + k) % shares) for i in range(shares)])  0.86 us
  transfers between devices with their start and end apart: 5, of which 2 were waited for; matrix products, arithmetic and copies ran while one was open for 0% of the time, Pallas kernels for 40%

profile of v3, /device:TPU:0, one launch (start us, length us, event | category | flops | bytes accessed | tf_op | source)
XLA Modules:
  0.0 17.4 jit_solution(3808686383707460899)
XLA Ops:
  0.0 0.0 copy-start
  0.0 0.0 copy-start.1
  0.0 1.1 %copy-done.1 = bf16[2,120,1024]{2,1,0:T(8,128)(2,1)S(1)} copy-done((bf16[2,120,1024]{2,1,0:T(8,128)(2,1)S(1)}, bf16[2,120,1024]{2,1,0:T(8,128)(2,1)}, u32[]{:S(2)}) %copy-start.1) | copy-done | bytes 491544
  1.1 0.0 copy-start.2
  1.1 3.0 %collective-permute-start = (bf16[2,120,512]{2,1,0:T(8,128)(2,1)S(1)}, bf16[2,120,512]{2,1,0:T(8,128)(2,1)S(1)}, u32[]{:S(2)}, u32[]{:S(2)}) collective-permute-start(bf16[2,120,512]{2,1,0:T(8,128)(2,1)S(1)} %get-tuple-element.29), channel_id=1, source_target_pairs={{0,1},{1,0},{2,3},{3,2},{4,5},{5,4},{6,7},{7,6},{8,9},{9,8},{10,11... | collective-permute-start | bytes 737288 | tf_op jit(solution)/shard_map/ppermute | solution.py:341
  4.1 0.0 copy-done
  4.1 0.0 copy-start.5
  4.1 0.0 copy-start.6
  4.2 0.0 copy-start.3
  4.2 0.1 collective-permute-start.1
  4.3 0.0 copy-start.4
  4.3 0.1 collective-permute-start.2
  4.4 0.0 copy-done.2
  4.4 0.4 %copy-done.5 = s32[2,2]{1,0:T(2,128)S(1)} copy-done((s32[2,2]{1,0:T(2,128)S(1)}, s32[2,2]{1,0:T(2,128)}, u32[]{:S(2)}) %copy-start.5) | copy-done | bytes 40
  4.8 0.0 copy-done.6
  4.8 0.0 copy-done.3
  4.9 0.1 copy-done.4
  5.0 0.5 %setup.1 = (bf16[9,96,128]{2,1,0:T(8,128)(2,1)S(1)}, bf16[9,32,128]{2,1,0:T(8,128)(2,1)S(1)}, bf16[9,128,128]{2,1,0:T(8,128)(2,1)S(1)}, f32[2,5,8,128]{3,2,1,0:T...) custom-call(bf16[9,2,23]{2,1,0:T(2,128)(2,1)S(1)} %copy-done.3, ...), custom_call_target="tpu_custom_call" | custom-call | flops 500000000 | bytes 1500000 | tf_op jit(solution)/shard_map/setup/pallas_call | solution.py:329
  5.5 0.1 collective-permute-done.1.near
  5.5 2.1 %first.3 = (bf16[2,88,512]{2,1,0:T(8,128)(2,1)S(1)}, bf16[2,5,48,640]{3,2,1,0:T(8,128)(2,1)S(1)}) custom-call(bf16[2,120,1024]{2,1,0:T(8,128)(2,1)S(1)} %copy-done, f32[2,5,8,128]{3,2,1,0:T(8,128)S(1)} %get-tuple-element.33.active, f32[2,120,128]{2,1,0:T(8,128)S(1)} %get-tuple-element.34.covered, bf16[192,128]{1,0:T(8,128)(2,1)S(1)} %get-tuple-element.35.features, ...), custom_call_target="tpu_custom_call" | custom-call | flops 10000000 | bytes 30000 | tf_op jit(solution)/shard_map/first/pallas_call | solution.py:329
  7.6 1.5 %collective-permute-start.4 = (bf16[2,88,512]{2,1,0:T(8,128)(2,1)S(1)}, bf16[2,88,512]{2,1,0:T(8,128)(2,1)S(1)}, u32[]{:S(2)}, u32[]{:S(2)}) collective-permute-start(bf16[2,88,512]{2,1,0:T(8,128)(2,1)S(1)} %get-tuple-element.50), channel_id=1, source_target_pairs={{0,1},{1,0},{2,3},{3,2},{4,5},{5,4},{6,7},{7,6},{8,9},{9,8},{10,11... | collective-permute-start | bytes 540680 | tf_op jit(solution)/shard_map/ppermute | solution.py:341
  9.1 2.0 %first.2 = (bf16[2,88,512]{2,1,0:T(8,128)(2,1)S(1)}, bf16[2,5,48,640]{3,2,1,0:T(8,128)(2,1)S(1)}) custom-call(bf16[2,120,1024]{2,1,0:T(8,128)(2,1)S(1)} %copy-done, f32[2,5,8,128]{3,2,1,0:T(8,128)S(1)} %get-tuple-element.33.active, f32[2,120,128]{2,1,0:T(8,128)S(1)} %get-tuple-element.34.covered, bf16[192,128]{1,0:T(8,128)(2,1)S(1)} %get-tuple-element.35.features, ...), custom_call_target="tpu_custom_call" | custom-call | flops 1500000000 | bytes 4500000 | tf_op jit(solution)/shard_map/first/pallas_call | solution.py:329
  11.1 0.0 collective-permute-done.refs_3_
  11.1 0.0 collective-permute-done.2.far
  11.1 1.0 %second.2 = bf16[2,32,512]{2,1,0:T(8,128)(2,1)S(1)} custom-call(bf16[2,120,1024]{2,1,0:T(8,128)(2,1)S(1)} %copy-done, bf16[2,16,1024]{2,1,0:T(8,128)(2,1)S(1)} %collective-permute-done.1.near, bf16[2,16,1024]{2,1,0:T(8,128)(2,1)S(1)} %collective-permute-done.2.far, f32[2,120,128]{2,1,0:T(8,128)S(1)} %get-tuple-element.34.covered, ...), custom_call_target="tpu_custom_call" | custom-call | flops 10000000 | bytes 30000 | tf_op jit(solution)/shard_map/second/pallas_call | solution.py:329
  12.1 2.1 %collective-permute-start.3 = (bf16[2,32,512]{2,1,0:T(8,128)(2,1)S(1)}, bf16[2,32,512]{2,1,0:T(8,128)(2,1)S(1)}, u32[]{:S(2)}, u32[]{:S(2)}) collective-permute-start(bf16[2,32,512]{2,1,0:T(8,128)(2,1)S(1)} %second.2), channel_id=1, source_target_pairs={{0,1},{1,0},{2,3},{3,2},{4,5},{5,4},{6,7},{7,6},{8,9},{9,8},{10,11... | collective-permute-start | bytes 196616 | tf_op jit(solution)/shard_map/ppermute | solution.py:341
  14.2 0.9 %second.3.refs_0_ = bf16[2,32,512]{2,1,0:T(8,128)(2,1)S(1)} custom-call(bf16[2,120,1024]{2,1,0:T(8,128)(2,1)S(1)} %copy-done, bf16[2,16,1024]{2,1,0:T(8,128)(2,1)S(1)} %collective-permute-done.1.near, bf16[2,16,1024]{2,1,0:T(8,128)(2,1)S(1)} %collective-permute-done.2.far, f32[2,120,128]{2,1,0:T(8,128)S(1)} %get-tuple-element.34.covered, ...), custom_call_target="tpu_custom_call" | custom-call | flops 10000000 | bytes 30000 | tf_op jit(solution)/shard_map/second/pallas_call | solution.py:329
  15.2 0.0 collective-permute-done.4.refs_1_
  15.2 0.4 %first_coadd.1.refs_4_ = f32[88,512]{1,0:T(8,128)S(1)} custom-call(bf16[2,88,512]{2,1,0:T(8,128)(2,1)S(1)} %get-tuple-element.49.refs_0_, bf16[2,88,512]{2,1,0:T(8,128)(2,1)S(1)} %collective-permute-done.4.refs_1_, bf16[2,120,512]{2,1,0:T(8,128)(2,1)S(1)} %get-tuple-element.47.refs_2_, bf16[2,120,512]{2,1,0:T(8,128)(2,1)S(1)} %collective-permute-done.refs_3_), custom_call_target="tpu_custom_call" | custom-call | flops 10000000 | bytes 30000 | tf_op jit(solution)/shard_map/first_coadd/pallas_call | solution.py:329
  15.6 0.9 %collective-permute-done.3.refs_1_ = bf16[2,32,512]{2,1,0:T(8,128)(2,1)S(1)} collective-permute-done((bf16[2,32,512]{2,1,0:T(8,128)(2,1)S(1)}, bf16[2,32,512]{2,1,0:T(8,128)(2,1)S(1)}, u32[]{:S(2)}, u32[]{:S(2)}) %collective-permute-start.3) | collective-permute-done | bytes 65568 | tf_op jit(solution)/shard_map/ppermute | solution.py:341
  16.5 0.9 %second_coadd.1 = f32[120,512]{1,0:T(8,128)} custom-call(bf16[2,32,512]{2,1,0:T(8,128)(2,1)S(1)} %second.3.refs_0_, bf16[2,32,512]{2,1,0:T(8,128)(2,1)S(1)} %collective-permute-done.3.refs_1_, bf16[2,120,512]{2,1,0:T(8,128)(2,1)S(1)} %get-tuple-element.47.refs_2_, bf16[2,120,512]{2,1,0:T(8,128)(2,1)S(1)} %collective-permute-done.refs_3_, ...), custom_call_target="tpu_custom_call" | custom-call | flops 10000000 | bytes 30000 | tf_op jit(solution)/shard_map/second_coadd/pallas_call | solution.py:329
  (2 shorter events, 0.1 us)
Async XLA Ops:
  0.0 4.1 %copy-start = (bf16[2,120,1024]{2,1,0:T(8,128)(2,1)S(1)}, bf16[2,120,1024]{2,1,0:T(8,128)(2,1)}, u32[]{:S(2)}) copy-start(bf16[2,120,1024]{2,1,0:T(8,128)(2,1)} %warped.9) | copy-start | bytes 1474564
  0.0 1.1 %copy-start.1 = (bf16[2,120,1024]{2,1,0:T(8,128)(2,1)S(1)}, bf16[2,120,1024]{2,1,0:T(8,128)(2,1)}, u32[]{:S(2)}) copy-start(bf16[2,120,1024]{2,1,0:T(8,128)(2,1)} %variance.3) | copy-start | bytes 1474564
  1.1 3.3 %copy-start.2 = (f32[2,9,10]{2,0,1:T(2,128)S(1)}, f32[2,9,10]{2,0,1:T(2,128)}, u32[]{:S(2)}) copy-start(f32[2,9,10]{2,0,1:T(2,128)} %param.10) | copy-start | bytes 2164
  1.1 10.0 %collective-permute-start = (bf16[2,120,512]{2,1,0:T(8,128)(2,1)S(1)}, bf16[2,120,512]{2,1,0:T(8,128)(2,1)S(1)}, u32[]{:S(2)}, u32[]{:S(2)}) collective-permute-start(bf16[2,120,512]{2,1,0:T(8,128)(2,1)S(1)} %get-tuple-element.29), channel_id=1, source_target_pairs={{0,1},{1,0},{2,3},{3,2},{4,5},{5,4},{6,7},{7,6},{8,9},{9,8},{10,11... | collective-permute-start | bytes 737288 | tf_op jit(solution)/shard_map/ppermute | solution.py:341
  4.1 0.7 %copy-start.5 = (s32[2,2]{1,0:T(2,128)S(1)}, s32[2,2]{1,0:T(2,128)}, u32[]{:S(2)}) copy-start(s32[2,2]{1,0:T(2,128)} %footprint.1) | copy-start | bytes 52
  4.1 0.7 %copy-start.6 = (s32[2,8]{1,0:T(2,128)S(1)}, s32[2,8]{1,0:T(2,128)}, u32[]{:S(2)}) copy-start(s32[2,8]{1,0:T(2,128)} %masks.1) | copy-start | bytes 196
  4.2 0.7 %copy-start.3 = (bf16[9,2,23]{2,1,0:T(2,128)(2,1)S(1)}, bf16[9,2,23]{2,1,0:T(2,128)(2,1)}, u32[]{:S(2)}) copy-start(bf16[9,2,23]{2,1,0:T(2,128)(2,1)} %taps.1) | copy-start | bytes 2488
  4.2 1.3 %collective-permute-start.1 = (bf16[2,16,1024]{2,1,0:T(8,128)(2,1)S(1)}, bf16[2,16,1024]{2,1,0:T(8,128)(2,1)S(1)}, u32[]{:S(2)}, u32[]{:S(2)}) collective-permute-start(bf16[2,16,1024]{2,1,0:T(8,128)(2,1)S(1)} %get-tuple-element.31), channel_id=1, source_target_pairs={{0,2},{2,0},{4,6},{6,4},{8,10},{10,8},{12,14},{14,12},{16,18},{18,... | collective-permute-start | bytes 196616 | tf_op jit(solution)/shard_map/ppermute | solution.py:348
  4.3 0.7 %copy-start.4 = (s32[2,9]{1,0:T(2,128)S(1)}, s32[2,9]{1,0:T(2,128)}, u32[]{:S(2)}) copy-start(s32[2,9]{1,0:T(2,128)} %degrees.1) | copy-start | bytes 220
  4.3 6.8 %collective-permute-start.2 = (bf16[2,16,1024]{2,1,0:T(8,128)(2,1)S(1)}, bf16[2,16,1024]{2,1,0:T(8,128)(2,1)S(1)}, u32[]{:S(2)}, u32[]{:S(2)}) collective-permute-start(bf16[2,16,1024]{2,1,0:T(8,128)(2,1)S(1)} %get-tuple-element.40), channel_id=1, source_target_pairs={{0,1},{1,0},{2,4},{3,5},{4,2},{5,3},{6,8},{7,9},{8,6},{9,7},{10,12... | collective-permute-start | bytes 196616 | tf_op jit(solution)/shard_map/ppermute | solution.py:356
  7.6 7.6 %collective-permute-start.4 = (bf16[2,88,512]{2,1,0:T(8,128)(2,1)S(1)}, bf16[2,88,512]{2,1,0:T(8,128)(2,1)S(1)}, u32[]{:S(2)}, u32[]{:S(2)}) collective-permute-start(bf16[2,88,512]{2,1,0:T(8,128)(2,1)S(1)} %get-tuple-element.50), channel_id=1, source_target_pairs={{0,1},{1,0},{2,3},{3,2},{4,5},{5,4},{6,7},{7,6},{8,9},{9,8},{10,11... | collective-permute-start | bytes 540680 | tf_op jit(solution)/shard_map/ppermute | solution.py:341
  12.1 4.4 %collective-permute-start.3 = (bf16[2,32,512]{2,1,0:T(8,128)(2,1)S(1)}, bf16[2,32,512]{2,1,0:T(8,128)(2,1)S(1)}, u32[]{:S(2)}, u32[]{:S(2)}) collective-permute-start(bf16[2,32,512]{2,1,0:T(8,128)(2,1)S(1)} %second.2), channel_id=1, source_target_pairs={{0,1},{1,0},{2,3},{3,2},{4,5},{5,4},{6,7},{7,6},{8,9},{9,8},{10,11... | collective-permute-start | bytes 196616 | tf_op jit(solution)/shard_map/ppermute | solution.py:341

commit v4 on v3

--- a/solution.py
+++ b/solution.py
@@ -11,6 +11,7 @@
 TERM = {power: index for index, power in enumerate(POWERS)}
 ROWS_PER_WORD = 15
 EDGE = 16
+SENT = 12
 LANES = 128
 GROUP = 3
 PIECES = 6
@@ -38,13 +39,16 @@
 
 
 def edges_kernel(warped, near, far):
-    row_count = warped.shape[1]
+    exp_count, row_count, _ = warped.shape
     even = lax.rem(lax.axis_index("sky"), 2) == 0
-    for e in range(warped.shape[0]):
+    heads, tails = [], []
+    for e in range(exp_count):
         image = warped[e].astype(F32)
-        head, tail = image[:EDGE], image[row_count - EDGE :]
-        near[e] = jnp.where(even, tail, head).astype(BF16)
-        far[e] = jnp.where(even, head, tail).astype(BF16)
+        heads.append(image[:SENT])
+        tails.append(image[row_count - SENT :])
+    head, tail = jnp.concatenate(heads, axis=0), jnp.concatenate(tails, axis=0)
+    near[...] = jnp.where(even, tail, head).astype(BF16)
+    far[...] = jnp.where(even, head, tail).astype(BF16)
 
 
 def pieces(value):
@@ -250,12 +254,13 @@
 
         def read(at, count):
             own = warped[e, :, pl.ds(at, count)].astype(F32)
-            same = near[e, :, pl.ds(at, count)].astype(F32)
-            other = far[e, :, pl.ds(at, count)].astype(F32)
+            same = near[:, pl.ds(at, count)].astype(F32)[e * SENT : (e + 1) * SENT]
+            other = far[:, pl.ds(at, count)].astype(F32)[e * SENT : (e + 1) * SENT]
             up, down = jnp.where(even, other, same), jnp.where(even, same, other)
             up = jnp.where(sky > 0, up, 0.0)
             down = jnp.where(sky < lax.axis_size("sky") - 1, down, 0.0)
-            return jnp.concatenate([up, own[:span], own[row_count - span :], down], axis=0)
+            gap = jnp.zeros((EDGE - SENT, count), F32)
+            return jnp.concatenate([gap, up, own[:span], own[row_count - span :], down, gap], axis=0)
 
         strip[e] = windows_of(read, start, width, col_count, parts, half)
         rows[e] = jnp.dot(band, strip[e], preferred_element_type=F32).astype(BF16)
@@ -291,11 +296,13 @@
 
 
 def second_coadd_kernel(shares, *refs):
-    fields, variances, done, coadd = refs[:shares], refs[shares : 2 * shares], refs[-2], refs[-1]
+    fields, variances, done = refs[:shares], refs[shares : 2 * shares], refs[2 * shares]
+    coadd, edges, copied = refs[2 * shares + 1 :]
     exp_count, row_count, width = variances[0].shape
     size = done.shape[0]
     pairs = [(k, e) for k in range(shares) for e in range(exp_count)]
-    coadd[EDGE : EDGE + size] = done[...]
+    inner = pltpu.make_async_copy(done, coadd.at[EDGE : EDGE + size], copied.at[0])
+    inner.start()
     for at in range(0, width, LANES):
         span = slice(at, at + LANES)
         values = [fields[k][e, :, span].astype(F32) for k, e in pairs]
@@ -303,9 +310,14 @@
         for k, e in pairs:
             spread = variances[k][e, :, span].astype(F32)
             spreads.append(jnp.concatenate([spread[:EDGE], spread[row_count - EDGE :]], axis=0))
-        result = robust_sum(values, spreads)
-        coadd[:EDGE, span] = result[:EDGE]
-        coadd[row_count - EDGE :, span] = result[EDGE:]
+        edges[:, span] = robust_sum(values, spreads)
+    upper = pltpu.make_async_copy(edges.at[:EDGE], coadd.at[:EDGE], copied.at[1])
+    lower = pltpu.make_async_copy(edges.at[EDGE:], coadd.at[row_count - EDGE :], copied.at[2])
+    upper.start()
+    lower.start()
+    inner.wait()
+    upper.wait()
+    lower.wait()
 
 
 def body(warped, variance, basis_taps, coeffs, degrees, footprint, masks):
@@ -343,7 +355,7 @@
     variances = call(variance_kernel, "variance", [array(exp_count, row_count, width)] * shares, variance)
     variances = [variances[0]] + [to_share(variances[k], k) for k in range(1, shares)]
 
-    edge = array(exp_count, EDGE, col_count)
+    edge = array(exp_count * SENT, col_count)
     near, far = call(edges_kernel, "edges", [edge, edge], warped)
     near = lax.ppermute(near, "sky", [(i, i ^ 1) for i in range(sky_count) if i ^ 1 < sky_count])
     partner = {i: i + 1 if i % 2 else i - 1 for i in range(1, sky_count)}
@@ -437,15 +449,15 @@
         *variances,
         cost=0.01,
     )
-    return call(
+    return pl.pallas_call(
         functools.partial(second_coadd_kernel, shares),
-        "second_coadd",
-        array(row_count, width, dtype=F32),
-        *seconds,
-        *variances,
-        done,
-        cost=0.01,
-    )
+        out_shape=array(row_count, width, dtype=F32),
+        in_specs=[vmem] * (2 * shares + 1),
+        out_specs=pl.BlockSpec(memory_space=pl.ANY),
+        scratch_shapes=[pltpu.VMEM((2 * EDGE, width), F32), pltpu.SemaphoreType.DMA((3,))],
+        compiler_params=pltpu.CompilerParams(vmem_limit_bytes=8 * 2**20),
+        name="second_coadd",
+    )(*seconds, *variances, done)
 
 
 def solution(mesh):

time: 17.5 us -> 17.4 us (level)
  starting transfers between devices: 6.79 us -> 6.46 us
  waiting for transfers between devices: 0.93 us -> 1.25 us
    pallas_call x9 -> x8, Pallas kernels: 7.86 us -> 6.98 us  [call(): pl.pallas_call(kernel, out_shape=out_shape, in_specs=[vmem] * len(operand...]
    pallas_call x0 -> x1, Pallas kernels: none -> 0.82 us  [body(): pl.pallas_call(functools.partial(second_coadd_kernel, shares), out_shape=...]
    ppermute x3, waiting for transfers between devices: 0.86 us -> 1.21 us  [to_share(): lax.ppermute(values, 'exp', [(i, (i + k) % shares) for i in range(shares)])]
    ppermute x3, starting transfers between devices: 6.61 us -> 6.28 us  [to_share(): lax.ppermute(values, 'exp', [(i, (i + k) % shares) for i in range(shares)])]
where the time goes in v4:
time: 17.4 us; the launch traced here: 17.3 us
  Pallas kernels  7.81 us (45%)
  starting transfers between devices  6.46 us (37%)
  local copies, waits for them, and re-layouts  1.66 us (10%)
  waiting for transfers between devices  1.25 us (7%)
    pallas_call x8, Pallas kernels, call(): pl.pallas_call(kernel, out_shape=out_shape, in_specs=[vmem] * len(operand...  6.98 us
    ppermute x3, starting transfers between devices, to_share(): lax.ppermute(values, 'exp', [(i, (i + k) % shares) for i in range(shares)])  6.28 us
    unnamed x14, local copies, waits for them, and re-layouts  1.66 us
    ppermute x3, waiting for transfers between devices, to_share(): lax.ppermute(values, 'exp', [(i, (i + k) % shares) for i in range(shares)])  1.21 us
    pallas_call x1, Pallas kernels, body(): pl.pallas_call(functools.partial(second_coadd_kernel, shares), out_shape=...  0.82 us
  transfers between devices with their start and end apart: 5, of which 2 were waited for; matrix products, arithmetic and copies ran while one was open for 0% of the time, Pallas kernels for 40%

profile of v4, /device:TPU:0, one launch (start us, length us, event | category | flops | bytes accessed | tf_op | source)
XLA Modules:
  0.0 17.3 jit_solution(12976508731030423424)
XLA Ops:
  0.0 0.0 copy-start
  0.0 0.0 copy-start.1
  0.0 1.1 %copy-done.1 = bf16[2,120,1024]{2,1,0:T(8,128)(2,1)S(1)} copy-done((bf16[2,120,1024]{2,1,0:T(8,128)(2,1)S(1)}, bf16[2,120,1024]{2,1,0:T(8,128)(2,1)}, u32[]{:S(2)}) %copy-start.1) | copy-done | bytes 491544
  1.1 0.0 copy-start.2
  1.1 3.0 %collective-permute-start = (bf16[2,120,512]{2,1,0:T(8,128)(2,1)S(1)}, bf16[2,120,512]{2,1,0:T(8,128)(2,1)S(1)}, u32[]{:S(2)}, u32[]{:S(2)}) collective-permute-start(bf16[2,120,512]{2,1,0:T(8,128)(2,1)S(1)} %get-tuple-element.29), channel_id=1, source_target_pairs={{0,1},{1,0},{2,3},{3,2},{4,5},{5,4},{6,7},{7,6},{8,9},{9,8},{10,11... | collective-permute-start | bytes 737288 | tf_op jit(solution)/shard_map/ppermute | solution.py:353
  4.1 0.0 copy-done
  4.1 0.0 copy-start.5
  4.1 0.0 copy-start.6
  4.2 0.0 copy-start.3
  4.2 0.1 collective-permute-start.1
  4.3 0.0 copy-start.4
  4.3 0.1 collective-permute-start.2
  4.4 0.0 copy-done.2
  4.4 0.4 %copy-done.5 = s32[2,2]{1,0:T(2,128)S(1)} copy-done((s32[2,2]{1,0:T(2,128)S(1)}, s32[2,2]{1,0:T(2,128)}, u32[]{:S(2)}) %copy-start.5) | copy-done | bytes 40
  4.8 0.0 copy-done.6
  4.8 0.0 copy-done.3
  4.9 0.1 copy-done.4
  5.0 0.5 %setup.1 = (bf16[9,96,128]{2,1,0:T(8,128)(2,1)S(1)}, bf16[9,32,128]{2,1,0:T(8,128)(2,1)S(1)}, bf16[9,128,128]{2,1,0:T(8,128)(2,1)S(1)}, f32[2,5,8,128]{3,2,1,0:T...) custom-call(bf16[9,2,23]{2,1,0:T(2,128)(2,1)S(1)} %copy-done.3, ...), custom_call_target="tpu_custom_call" | custom-call | flops 500000000 | bytes 1500000 | tf_op jit(solution)/shard_map/setup/pallas_call | solution.py:341
  5.5 0.0 collective-permute-done.1.near
  5.5 2.1 %first.3 = (bf16[2,88,512]{2,1,0:T(8,128)(2,1)S(1)}, bf16[2,5,48,640]{3,2,1,0:T(8,128)(2,1)S(1)}) custom-call(bf16[2,120,1024]{2,1,0:T(8,128)(2,1)S(1)} %copy-done, f32[2,5,8,128]{3,2,1,0:T(8,128)S(1)} %get-tuple-element.33.active, f32[2,120,128]{2,1,0:T(8,128)S(1)} %get-tuple-element.34.covered, bf16[192,128]{1,0:T(8,128)(2,1)S(1)} %get-tuple-element.35.features, ...), custom_call_target="tpu_custom_call" | custom-call | flops 10000000 | bytes 30000 | tf_op jit(solution)/shard_map/first/pallas_call | solution.py:341
  7.6 1.5 %collective-permute-start.4 = (bf16[2,88,512]{2,1,0:T(8,128)(2,1)S(1)}, bf16[2,88,512]{2,1,0:T(8,128)(2,1)S(1)}, u32[]{:S(2)}, u32[]{:S(2)}) collective-permute-start(bf16[2,88,512]{2,1,0:T(8,128)(2,1)S(1)} %get-tuple-element.50), channel_id=1, source_target_pairs={{0,1},{1,0},{2,3},{3,2},{4,5},{5,4},{6,7},{7,6},{8,9},{9,8},{10,11... | collective-permute-start | bytes 540680 | tf_op jit(solution)/shard_map/ppermute | solution.py:353
  9.1 2.0 %first.2 = (bf16[2,88,512]{2,1,0:T(8,128)(2,1)S(1)}, bf16[2,5,48,640]{3,2,1,0:T(8,128)(2,1)S(1)}) custom-call(bf16[2,120,1024]{2,1,0:T(8,128)(2,1)S(1)} %copy-done, f32[2,5,8,128]{3,2,1,0:T(8,128)S(1)} %get-tuple-element.33.active, f32[2,120,128]{2,1,0:T(8,128)S(1)} %get-tuple-element.34.covered, bf16[192,128]{1,0:T(8,128)(2,1)S(1)} %get-tuple-element.35.features, ...), custom_call_target="tpu_custom_call" | custom-call | flops 1500000000 | bytes 4500000 | tf_op jit(solution)/shard_map/first/pallas_call | solution.py:341
  11.1 0.0 collective-permute-done.refs_3_
  11.1 0.0 collective-permute-done.2.far
  11.1 1.0 %second.2 = bf16[2,32,512]{2,1,0:T(8,128)(2,1)S(1)} custom-call(bf16[2,120,1024]{2,1,0:T(8,128)(2,1)S(1)} %copy-done, bf16[24,1024]{1,0:T(8,128)(2,1)S(1)} %collective-permute-done.1.near, bf16[24,1024]{1,0:T(8,128)(2,1)S(1)} %collective-permute-done.2.far, f32[2,120,128]{2,1,0:T(8,128)S(1)} %get-tuple-element.34.covered, ...), custom_call_target="tpu_custom_call" | custom-call | flops 10000000 | bytes 30000 | tf_op jit(solution)/shard_map/second/pallas_call | solution.py:341
  12.1 1.8 %collective-permute-start.3 = (bf16[2,32,512]{2,1,0:T(8,128)(2,1)S(1)}, bf16[2,32,512]{2,1,0:T(8,128)(2,1)S(1)}, u32[]{:S(2)}, u32[]{:S(2)}) collective-permute-start(bf16[2,32,512]{2,1,0:T(8,128)(2,1)S(1)} %second.2), channel_id=1, source_target_pairs={{0,1},{1,0},{2,3},{3,2},{4,5},{5,4},{6,7},{7,6},{8,9},{9,8},{10,11... | collective-permute-start | bytes 196616 | tf_op jit(solution)/shard_map/ppermute | solution.py:353
  13.9 0.9 %second.3.refs_0_ = bf16[2,32,512]{2,1,0:T(8,128)(2,1)S(1)} custom-call(bf16[2,120,1024]{2,1,0:T(8,128)(2,1)S(1)} %copy-done, bf16[24,1024]{1,0:T(8,128)(2,1)S(1)} %collective-permute-done.1.near, bf16[24,1024]{1,0:T(8,128)(2,1)S(1)} %collective-permute-done.2.far, f32[2,120,128]{2,1,0:T(8,128)S(1)} %get-tuple-element.34.covered, ...), custom_call_target="tpu_custom_call" | custom-call | flops 10000000 | bytes 30000 | tf_op jit(solution)/shard_map/second/pallas_call | solution.py:341
  14.8 0.2 collective-permute-done.4.refs_1_
  15.0 0.4 %first_coadd.1.refs_4_ = f32[88,512]{1,0:T(8,128)S(1)} custom-call(bf16[2,88,512]{2,1,0:T(8,128)(2,1)S(1)} %get-tuple-element.49.refs_0_, bf16[2,88,512]{2,1,0:T(8,128)(2,1)S(1)} %collective-permute-done.4.refs_1_, bf16[2,120,512]{2,1,0:T(8,128)(2,1)S(1)} %get-tuple-element.47.refs_2_, bf16[2,120,512]{2,1,0:T(8,128)(2,1)S(1)} %collective-permute-done.refs_3_), custom_call_target="tpu_custom_call" | custom-call | flops 10000000 | bytes 30000 | tf_op jit(solution)/shard_map/first_coadd/pallas_call | solution.py:341
  15.4 1.0 %collective-permute-done.3.refs_1_ = bf16[2,32,512]{2,1,0:T(8,128)(2,1)S(1)} collective-permute-done((bf16[2,32,512]{2,1,0:T(8,128)(2,1)S(1)}, bf16[2,32,512]{2,1,0:T(8,128)(2,1)S(1)}, u32[]{:S(2)}, u32[]{:S(2)}) %collective-permute-start.3) | collective-permute-done | bytes 65568 | tf_op jit(solution)/shard_map/ppermute | solution.py:353
  16.5 0.8 %second_coadd.1 = f32[120,512]{1,0:T(8,128)} custom-call(bf16[2,32,512]{2,1,0:T(8,128)(2,1)S(1)} %second.3.refs_0_, bf16[2,32,512]{2,1,0:T(8,128)(2,1)S(1)} %collective-permute-done.3.refs_1_, bf16[2,120,512]{2,1,0:T(8,128)(2,1)S(1)} %get-tuple-element.47.refs_2_, bf16[2,120,512]{2,1,0:T(8,128)(2,1)S(1)} %collective-permute-done.refs_3_, ...), custom_call_target="tpu_custom_call" | custom-call | tf_op jit(solution)/shard_map/second_coadd/pallas_call | solution.py:452
  (2 shorter events, 0.1 us)
Async XLA Ops:
  0.0 4.1 %copy-start = (bf16[2,120,1024]{2,1,0:T(8,128)(2,1)S(1)}, bf16[2,120,1024]{2,1,0:T(8,128)(2,1)}, u32[]{:S(2)}) copy-start(bf16[2,120,1024]{2,1,0:T(8,128)(2,1)} %warped.9) | copy-start | bytes 1474564
  0.0 1.1 %copy-start.1 = (bf16[2,120,1024]{2,1,0:T(8,128)(2,1)S(1)}, bf16[2,120,1024]{2,1,0:T(8,128)(2,1)}, u32[]{:S(2)}) copy-start(bf16[2,120,1024]{2,1,0:T(8,128)(2,1)} %variance.3) | copy-start | bytes 1474564
  1.1 3.3 %copy-start.2 = (f32[2,9,10]{2,0,1:T(2,128)S(1)}, f32[2,9,10]{2,0,1:T(2,128)}, u32[]{:S(2)}) copy-start(f32[2,9,10]{2,0,1:T(2,128)} %param.10) | copy-start | bytes 2164
  1.1 10.0 %collective-permute-start = (bf16[2,120,512]{2,1,0:T(8,128)(2,1)S(1)}, bf16[2,120,512]{2,1,0:T(8,128)(2,1)S(1)}, u32[]{:S(2)}, u32[]{:S(2)}) collective-permute-start(bf16[2,120,512]{2,1,0:T(8,128)(2,1)S(1)} %get-tuple-element.29), channel_id=1, source_target_pairs={{0,1},{1,0},{2,3},{3,2},{4,5},{5,4},{6,7},{7,6},{8,9},{9,8},{10,11... | collective-permute-start | bytes 737288 | tf_op jit(solution)/shard_map/ppermute | solution.py:353
  4.1 0.7 %copy-start.5 = (s32[2,2]{1,0:T(2,128)S(1)}, s32[2,2]{1,0:T(2,128)}, u32[]{:S(2)}) copy-start(s32[2,2]{1,0:T(2,128)} %footprint.1) | copy-start | bytes 52
  4.1 0.7 %copy-start.6 = (s32[2,8]{1,0:T(2,128)S(1)}, s32[2,8]{1,0:T(2,128)}, u32[]{:S(2)}) copy-start(s32[2,8]{1,0:T(2,128)} %masks.1) | copy-start | bytes 196
  4.2 0.7 %copy-start.3 = (bf16[9,2,23]{2,1,0:T(2,128)(2,1)S(1)}, bf16[9,2,23]{2,1,0:T(2,128)(2,1)}, u32[]{:S(2)}) copy-start(bf16[9,2,23]{2,1,0:T(2,128)(2,1)} %taps.1) | copy-start | bytes 2488
  4.2 1.3 %collective-permute-start.1 = (bf16[24,1024]{1,0:T(8,128)(2,1)S(1)}, bf16[24,1024]{1,0:T(8,128)(2,1)S(1)}, u32[]{:S(2)}, u32[]{:S(2)}) collective-permute-start(bf16[24,1024]{1,0:T(8,128)(2,1)S(1)} %get-tuple-element.31), channel_id=1, source_target_pairs={{0,2},{2,0},{4,6},{6,4},{8,10},{10,8},{12,14},{14,12},{16,18},{18,... | collective-permute-start | bytes 147464 | tf_op jit(solution)/shard_map/ppermute | solution.py:360
  4.3 0.7 %copy-start.4 = (s32[2,9]{1,0:T(2,128)S(1)}, s32[2,9]{1,0:T(2,128)}, u32[]{:S(2)}) copy-start(s32[2,9]{1,0:T(2,128)} %degrees.1) | copy-start | bytes 220
  4.3 6.8 %collective-permute-start.2 = (bf16[24,1024]{1,0:T(8,128)(2,1)S(1)}, bf16[24,1024]{1,0:T(8,128)(2,1)S(1)}, u32[]{:S(2)}, u32[]{:S(2)}) collective-permute-start(bf16[24,1024]{1,0:T(8,128)(2,1)S(1)} %get-tuple-element.40), channel_id=1, source_target_pairs={{0,1},{1,0},{2,4},{3,5},{4,2},{5,3},{6,8},{7,9},{8,6},{9,7},{10,12... | collective-permute-start | bytes 147464 | tf_op jit(solution)/shard_map/ppermute | solution.py:368
  7.6 7.4 %collective-permute-start.4 = (bf16[2,88,512]{2,1,0:T(8,128)(2,1)S(1)}, bf16[2,88,512]{2,1,0:T(8,128)(2,1)S(1)}, u32[]{:S(2)}, u32[]{:S(2)}) collective-permute-start(bf16[2,88,512]{2,1,0:T(8,128)(2,1)S(1)} %get-tuple-element.50), channel_id=1, source_target_pairs={{0,1},{1,0},{2,3},{3,2},{4,5},{5,4},{6,7},{7,6},{8,9},{9,8},{10,11... | collective-permute-start | bytes 540680 | tf_op jit(solution)/shard_map/ppermute | solution.py:353
  12.1 4.4 %collective-permute-start.3 = (bf16[2,32,512]{2,1,0:T(8,128)(2,1)S(1)}, bf16[2,32,512]{2,1,0:T(8,128)(2,1)S(1)}, u32[]{:S(2)}, u32[]{:S(2)}) collective-permute-start(bf16[2,32,512]{2,1,0:T(8,128)(2,1)S(1)} %second.2), channel_id=1, source_target_pairs={{0,1},{1,0},{2,3},{3,2},{4,5},{5,4},{6,7},{7,6},{8,9},{9,8},{10,11... | collective-permute-start | bytes 196616 | tf_op jit(solution)/shard_map/ppermute | solution.py:353

commit v5 on v4

--- a/solution.py
+++ b/solution.py
@@ -175,26 +175,28 @@
                 lines[e, pair, 32:48, span] = jnp.concatenate([middle, low], axis=0).astype(BF16)
 
 
-def weighted_sums(e, parts, lines, features, rows, col_band, size):
-    out = []
-    for first in range(0, len(parts), GROUP):
-        members = range(first, min(first + GROUP, len(parts)))
-        span = slice(first * LANES, (members[-1] + 1) * LANES)
-        totals = [None] * len(members)
-        for b in range(col_band.shape[0]):
-            odd = b % 2
-            if not odd:
-                field = jnp.dot(features[:, : 8 * PIECES], lines[e, b // 2, :, span], preferred_element_type=F32)
-            window = jnp.concatenate(
-                [rows[e, b * size : (b + 1) * size, s * LANES : (s + 1) * LANES] for s in members], axis=0
-            )
-            along = jnp.dot(window, col_band[b], preferred_element_type=F32)
-            for i in range(len(members)):
-                weight = field[odd * size : (odd + 1) * size, i * LANES : (i + 1) * LANES]
-                value = weight * along[i * size : (i + 1) * size]
-                totals[i] = value if b == 0 else totals[i] + value
-        out += totals
-    return out
+def weighted_sums(members, lines, features, rows, col_band, size):
+    spans = [slice(s * LANES, (s + 1) * LANES) for _, s in members]
+    exposures = sorted({e for e, _ in members})
+    totals = [None] * len(members)
+    for b in range(col_band.shape[0]):
+        odd = b % 2
+        if not odd:
+            fields = {}
+            for e in exposures:
+                own = [s for other, s in members if other == e]
+                columns = lines[e, b // 2, :, own[0] * LANES : (own[-1] + 1) * LANES]
+                product = jnp.dot(features[:, : 8 * PIECES], columns, preferred_element_type=F32)
+                for i, s in enumerate(own):
+                    fields[e, s] = product[:, i * LANES : (i + 1) * LANES]
+        window = jnp.concatenate(
+            [rows[e, b * size : (b + 1) * size, span] for (e, _), span in zip(members, spans)], axis=0
+        )
+        along = jnp.dot(window, col_band[b], preferred_element_type=F32)
+        for i, member in enumerate(members):
+            value = fields[member][odd * size : (odd + 1) * size] * along[i * size : (i + 1) * size]
+            totals[i] = value if b == 0 else totals[i] + value
+    return totals
 
 
 def joined(blocks, parts, width):
@@ -233,7 +235,10 @@
         strip[e] = windows_of(read, start, width, col_count, parts, half)
         rows[e] = jnp.dot(band, strip[e], preferred_element_type=F32).astype(BF16)
     for e in range(exp_count):
-        blocks = weighted_sums(e, parts, lines, features, rows, col_band, size)
+        blocks = []
+        for low in range(0, len(parts), GROUP):
+            members = [(e, s) for s in range(low, min(low + GROUP, len(parts)))]
+            blocks += weighted_sums(members, lines, features, rows, col_band, size)
         counts = jnp.concatenate([covered[e, EDGE : EDGE + inner]] * (width // LANES), axis=1) > 0
         matched[e] = jnp.where(counts, joined(blocks, parts, width)[:inner], jnp.inf).astype(BF16)
 
@@ -264,8 +269,10 @@
 
         strip[e] = windows_of(read, start, width, col_count, parts, half)
         rows[e] = jnp.dot(band, strip[e], preferred_element_type=F32).astype(BF16)
-    for e in range(exp_count):
-        blocks = weighted_sums(e, parts, lines, features, rows, col_band, size)
+    members = [(e, s) for e in range(exp_count) for s in range(len(parts))]
+    every = weighted_sums(members, lines, features, rows, col_band, size)
+    for e in range(exp_count):
+        blocks = every[e * len(parts) : (e + 1) * len(parts)]
         counts = jnp.concatenate([covered[e, :EDGE], covered[e, row_count - EDGE :]], axis=0)
         counts = jnp.concatenate([counts] * (width // LANES), axis=1) > 0
         matched[e] = jnp.where(counts, joined(blocks, parts, width), jnp.inf).astype(BF16)

time: 17.4 us -> 17.4 us (level)
  no operation moved by 1% of the time
where the time goes in v5:
time: 17.4 us; the launch traced here: 17.3 us
  Pallas kernels  7.77 us (45%)
  starting transfers between devices  6.46 us (37%)
  local copies, waits for them, and re-layouts  1.66 us (10%)
  waiting for transfers between devices  1.28 us (7%)
    pallas_call x8, Pallas kernels, call(): pl.pallas_call(kernel, out_shape=out_shape, in_specs=[vmem] * len(operand...  6.95 us
    ppermute x3, starting transfers between devices, to_share(): lax.ppermute(values, 'exp', [(i, (i + k) % shares) for i in range(shares)])  6.28 us
    unnamed x14, local copies, waits for them, and re-layouts  1.66 us
    ppermute x3, waiting for transfers between devices, to_share(): lax.ppermute(values, 'exp', [(i, (i + k) % shares) for i in range(shares)])  1.24 us
    pallas_call x1, Pallas kernels, body(): pl.pallas_call(functools.partial(second_coadd_kernel, shares), out_shape=...  0.82 us
  transfers between devices with their start and end apart: 5, of which 2 were waited for; matrix products, arithmetic and copies ran while one was open for 0% of the time, Pallas kernels for 40%

profile of v5, /device:TPU:0, one launch (start us, length us, event | category | flops | bytes accessed | tf_op | source)
XLA Modules:
  0.0 17.3 jit_solution(2282579375658342693)
XLA Ops:
  0.0 0.0 copy-start
  0.0 0.0 copy-start.1
  0.0 1.1 %copy-done.1 = bf16[2,120,1024]{2,1,0:T(8,128)(2,1)S(1)} copy-done((bf16[2,120,1024]{2,1,0:T(8,128)(2,1)S(1)}, bf16[2,120,1024]{2,1,0:T(8,128)(2,1)}, u32[]{:S(2)}) %copy-start.1) | copy-done | bytes 491544
  1.1 0.0 copy-start.2
  1.1 3.0 %collective-permute-start = (bf16[2,120,512]{2,1,0:T(8,128)(2,1)S(1)}, bf16[2,120,512]{2,1,0:T(8,128)(2,1)S(1)}, u32[]{:S(2)}, u32[]{:S(2)}) collective-permute-start(bf16[2,120,512]{2,1,0:T(8,128)(2,1)S(1)} %get-tuple-element.29), channel_id=1, source_target_pairs={{0,1},{1,0},{2,3},{3,2},{4,5},{5,4},{6,7},{7,6},{8,9},{9,8},{10,11... | collective-permute-start | bytes 737288 | tf_op jit(solution)/shard_map/ppermute | solution.py:360
  4.1 0.0 copy-done
  4.1 0.0 copy-start.5
  4.1 0.0 copy-start.6
  4.2 0.0 copy-start.3
  4.2 0.1 collective-permute-start.1
  4.3 0.0 copy-start.4
  4.3 0.1 collective-permute-start.2
  4.4 0.0 copy-done.2
  4.4 0.4 %copy-done.5 = s32[2,2]{1,0:T(2,128)S(1)} copy-done((s32[2,2]{1,0:T(2,128)S(1)}, s32[2,2]{1,0:T(2,128)}, u32[]{:S(2)}) %copy-start.5) | copy-done | bytes 40
  4.8 0.0 copy-done.6
  4.8 0.0 copy-done.3
  4.9 0.1 copy-done.4
  5.0 0.5 %setup.1 = (bf16[9,96,128]{2,1,0:T(8,128)(2,1)S(1)}, bf16[9,32,128]{2,1,0:T(8,128)(2,1)S(1)}, bf16[9,128,128]{2,1,0:T(8,128)(2,1)S(1)}, f32[2,5,8,128]{3,2,1,0:T...) custom-call(bf16[9,2,23]{2,1,0:T(2,128)(2,1)S(1)} %copy-done.3, ...), custom_call_target="tpu_custom_call" | custom-call | flops 500000000 | bytes 1500000 | tf_op jit(solution)/shard_map/setup/pallas_call | solution.py:348
  5.5 0.0 collective-permute-done.1.near
  5.5 2.1 %first.3 = (bf16[2,88,512]{2,1,0:T(8,128)(2,1)S(1)}, bf16[2,5,48,640]{3,2,1,0:T(8,128)(2,1)S(1)}) custom-call(bf16[2,120,1024]{2,1,0:T(8,128)(2,1)S(1)} %copy-done, f32[2,5,8,128]{3,2,1,0:T(8,128)S(1)} %get-tuple-element.33.active, f32[2,120,128]{2,1,0:T(8,128)S(1)} %get-tuple-element.34.covered, bf16[192,128]{1,0:T(8,128)(2,1)S(1)} %get-tuple-element.35.features, ...), custom_call_target="tpu_custom_call" | custom-call | flops 10000000 | bytes 30000 | tf_op jit(solution)/shard_map/first/pallas_call | solution.py:348
  7.6 1.5 %collective-permute-start.4 = (bf16[2,88,512]{2,1,0:T(8,128)(2,1)S(1)}, bf16[2,88,512]{2,1,0:T(8,128)(2,1)S(1)}, u32[]{:S(2)}, u32[]{:S(2)}) collective-permute-start(bf16[2,88,512]{2,1,0:T(8,128)(2,1)S(1)} %get-tuple-element.50), channel_id=1, source_target_pairs={{0,1},{1,0},{2,3},{3,2},{4,5},{5,4},{6,7},{7,6},{8,9},{9,8},{10,11... | collective-permute-start | bytes 540680 | tf_op jit(solution)/shard_map/ppermute | solution.py:360
  9.1 2.0 %first.2 = (bf16[2,88,512]{2,1,0:T(8,128)(2,1)S(1)}, bf16[2,5,48,640]{3,2,1,0:T(8,128)(2,1)S(1)}) custom-call(bf16[2,120,1024]{2,1,0:T(8,128)(2,1)S(1)} %copy-done, f32[2,5,8,128]{3,2,1,0:T(8,128)S(1)} %get-tuple-element.33.active, f32[2,120,128]{2,1,0:T(8,128)S(1)} %get-tuple-element.34.covered, bf16[192,128]{1,0:T(8,128)(2,1)S(1)} %get-tuple-element.35.features, ...), custom_call_target="tpu_custom_call" | custom-call | flops 1500000000 | bytes 4500000 | tf_op jit(solution)/shard_map/first/pallas_call | solution.py:348
  11.1 0.0 collective-permute-done.refs_3_
  11.1 0.0 collective-permute-done.2.far
  11.1 0.9 %second.2 = bf16[2,32,512]{2,1,0:T(8,128)(2,1)S(1)} custom-call(bf16[2,120,1024]{2,1,0:T(8,128)(2,1)S(1)} %copy-done, bf16[24,1024]{1,0:T(8,128)(2,1)S(1)} %collective-permute-done.1.near, bf16[24,1024]{1,0:T(8,128)(2,1)S(1)} %collective-permute-done.2.far, f32[2,120,128]{2,1,0:T(8,128)S(1)} %get-tuple-element.34.covered, ...), custom_call_target="tpu_custom_call" | custom-call | flops 10000000 | bytes 30000 | tf_op jit(solution)/shard_map/second/pallas_call | solution.py:348
  12.1 1.8 %collective-permute-start.3 = (bf16[2,32,512]{2,1,0:T(8,128)(2,1)S(1)}, bf16[2,32,512]{2,1,0:T(8,128)(2,1)S(1)}, u32[]{:S(2)}, u32[]{:S(2)}) collective-permute-start(bf16[2,32,512]{2,1,0:T(8,128)(2,1)S(1)} %second.2), channel_id=1, source_target_pairs={{0,1},{1,0},{2,3},{3,2},{4,5},{5,4},{6,7},{7,6},{8,9},{9,8},{10,11... | collective-permute-start | bytes 196616 | tf_op jit(solution)/shard_map/ppermute | solution.py:360
  13.9 0.9 %second.3.refs_0_ = bf16[2,32,512]{2,1,0:T(8,128)(2,1)S(1)} custom-call(bf16[2,120,1024]{2,1,0:T(8,128)(2,1)S(1)} %copy-done, bf16[24,1024]{1,0:T(8,128)(2,1)S(1)} %collective-permute-done.1.near, bf16[24,1024]{1,0:T(8,128)(2,1)S(1)} %collective-permute-done.2.far, f32[2,120,128]{2,1,0:T(8,128)S(1)} %get-tuple-element.34.covered, ...), custom_call_target="tpu_custom_call" | custom-call | flops 10000000 | bytes 30000 | tf_op jit(solution)/shard_map/second/pallas_call | solution.py:348
  14.8 0.2 %collective-permute-done.4.refs_1_ = bf16[2,88,512]{2,1,0:T(8,128)(2,1)S(1)} collective-permute-done((bf16[2,88,512]{2,1,0:T(8,128)(2,1)S(1)}, bf16[2,88,512]{2,1,0:T(8,128)(2,1)S(1)}, u32[]{:S(2)}, u32[]{:S(2)}) %collective-permute-start.4) | collective-permute-done | bytes 180256 | tf_op jit(solution)/shard_map/ppermute | solution.py:360
  15.0 0.4 %first_coadd.1.refs_4_ = f32[88,512]{1,0:T(8,128)S(1)} custom-call(bf16[2,88,512]{2,1,0:T(8,128)(2,1)S(1)} %get-tuple-element.49.refs_0_, bf16[2,88,512]{2,1,0:T(8,128)(2,1)S(1)} %collective-permute-done.4.refs_1_, bf16[2,120,512]{2,1,0:T(8,128)(2,1)S(1)} %get-tuple-element.47.refs_2_, bf16[2,120,512]{2,1,0:T(8,128)(2,1)S(1)} %collective-permute-done.refs_3_), custom_call_target="tpu_custom_call" | custom-call | flops 10000000 | bytes 30000 | tf_op jit(solution)/shard_map/first_coadd/pallas_call | solution.py:348
  15.4 1.0 %collective-permute-done.3.refs_1_ = bf16[2,32,512]{2,1,0:T(8,128)(2,1)S(1)} collective-permute-done((bf16[2,32,512]{2,1,0:T(8,128)(2,1)S(1)}, bf16[2,32,512]{2,1,0:T(8,128)(2,1)S(1)}, u32[]{:S(2)}, u32[]{:S(2)}) %collective-permute-start.3) | collective-permute-done | bytes 65568 | tf_op jit(solution)/shard_map/ppermute | solution.py:360
  16.5 0.8 %second_coadd.1 = f32[120,512]{1,0:T(8,128)} custom-call(bf16[2,32,512]{2,1,0:T(8,128)(2,1)S(1)} %second.3.refs_0_, bf16[2,32,512]{2,1,0:T(8,128)(2,1)S(1)} %collective-permute-done.3.refs_1_, bf16[2,120,512]{2,1,0:T(8,128)(2,1)S(1)} %get-tuple-element.47.refs_2_, bf16[2,120,512]{2,1,0:T(8,128)(2,1)S(1)} %collective-permute-done.refs_3_, ...), custom_call_target="tpu_custom_call" | custom-call | tf_op jit(solution)/shard_map/second_coadd/pallas_call | solution.py:459
  (2 shorter events, 0.1 us)
Async XLA Ops:
  0.0 4.1 %copy-start = (bf16[2,120,1024]{2,1,0:T(8,128)(2,1)S(1)}, bf16[2,120,1024]{2,1,0:T(8,128)(2,1)}, u32[]{:S(2)}) copy-start(bf16[2,120,1024]{2,1,0:T(8,128)(2,1)} %warped.9) | copy-start | bytes 1474564
  0.0 1.1 %copy-start.1 = (bf16[2,120,1024]{2,1,0:T(8,128)(2,1)S(1)}, bf16[2,120,1024]{2,1,0:T(8,128)(2,1)}, u32[]{:S(2)}) copy-start(bf16[2,120,1024]{2,1,0:T(8,128)(2,1)} %variance.3) | copy-start | bytes 1474564
  1.1 3.3 %copy-start.2 = (f32[2,9,10]{2,0,1:T(2,128)S(1)}, f32[2,9,10]{2,0,1:T(2,128)}, u32[]{:S(2)}) copy-start(f32[2,9,10]{2,0,1:T(2,128)} %param.10) | copy-start | bytes 2164
  1.1 10.0 %collective-permute-start = (bf16[2,120,512]{2,1,0:T(8,128)(2,1)S(1)}, bf16[2,120,512]{2,1,0:T(8,128)(2,1)S(1)}, u32[]{:S(2)}, u32[]{:S(2)}) collective-permute-start(bf16[2,120,512]{2,1,0:T(8,128)(2,1)S(1)} %get-tuple-element.29), channel_id=1, source_target_pairs={{0,1},{1,0},{2,3},{3,2},{4,5},{5,4},{6,7},{7,6},{8,9},{9,8},{10,11... | collective-permute-start | bytes 737288 | tf_op jit(solution)/shard_map/ppermute | solution.py:360
  4.1 0.7 %copy-start.5 = (s32[2,2]{1,0:T(2,128)S(1)}, s32[2,2]{1,0:T(2,128)}, u32[]{:S(2)}) copy-start(s32[2,2]{1,0:T(2,128)} %footprint.1) | copy-start | bytes 52
  4.1 0.7 %copy-start.6 = (s32[2,8]{1,0:T(2,128)S(1)}, s32[2,8]{1,0:T(2,128)}, u32[]{:S(2)}) copy-start(s32[2,8]{1,0:T(2,128)} %masks.1) | copy-start | bytes 196
  4.2 0.7 %copy-start.3 = (bf16[9,2,23]{2,1,0:T(2,128)(2,1)S(1)}, bf16[9,2,23]{2,1,0:T(2,128)(2,1)}, u32[]{:S(2)}) copy-start(bf16[9,2,23]{2,1,0:T(2,128)(2,1)} %taps.1) | copy-start | bytes 2488
  4.2 1.3 %collective-permute-start.1 = (bf16[24,1024]{1,0:T(8,128)(2,1)S(1)}, bf16[24,1024]{1,0:T(8,128)(2,1)S(1)}, u32[]{:S(2)}, u32[]{:S(2)}) collective-permute-start(bf16[24,1024]{1,0:T(8,128)(2,1)S(1)} %get-tuple-element.31), channel_id=1, source_target_pairs={{0,2},{2,0},{4,6},{6,4},{8,10},{10,8},{12,14},{14,12},{16,18},{18,... | collective-permute-start | bytes 147464 | tf_op jit(solution)/shard_map/ppermute | solution.py:367
  4.3 0.7 %copy-start.4 = (s32[2,9]{1,0:T(2,128)S(1)}, s32[2,9]{1,0:T(2,128)}, u32[]{:S(2)}) copy-start(s32[2,9]{1,0:T(2,128)} %degrees.1) | copy-start | bytes 220
  4.3 6.8 %collective-permute-start.2 = (bf16[24,1024]{1,0:T(8,128)(2,1)S(1)}, bf16[24,1024]{1,0:T(8,128)(2,1)S(1)}, u32[]{:S(2)}, u32[]{:S(2)}) collective-permute-start(bf16[24,1024]{1,0:T(8,128)(2,1)S(1)} %get-tuple-element.40), channel_id=1, source_target_pairs={{0,1},{1,0},{2,4},{3,5},{4,2},{5,3},{6,8},{7,9},{8,6},{9,7},{10,12... | collective-permute-start | bytes 147464 | tf_op jit(solution)/shard_map/ppermute | solution.py:375
  7.6 7.4 %collective-permute-start.4 = (bf16[2,88,512]{2,1,0:T(8,128)(2,1)S(1)}, bf16[2,88,512]{2,1,0:T(8,128)(2,1)S(1)}, u32[]{:S(2)}, u32[]{:S(2)}) collective-permute-start(bf16[2,88,512]{2,1,0:T(8,128)(2,1)S(1)} %get-tuple-element.50), channel_id=1, source_target_pairs={{0,1},{1,0},{2,3},{3,2},{4,5},{5,4},{6,7},{7,6},{8,9},{9,8},{10,11... | collective-permute-start | bytes 540680 | tf_op jit(solution)/shard_map/ppermute | solution.py:360
  12.1 4.4 %collective-permute-start.3 = (bf16[2,32,512]{2,1,0:T(8,128)(2,1)S(1)}, bf16[2,32,512]{2,1,0:T(8,128)(2,1)S(1)}, u32[]{:S(2)}, u32[]{:S(2)}) collective-permute-start(bf16[2,32,512]{2,1,0:T(8,128)(2,1)S(1)} %second.2), channel_id=1, source_target_pairs={{0,1},{1,0},{2,3},{3,2},{4,5},{5,4},{6,7},{7,6},{8,9},{9,8},{10,11... | collective-permute-start | bytes 196616 | tf_op jit(solution)/shard_map/ppermute | solution.py:360

commit v6 on v5

--- a/solution.py
+++ b/solution.py
@@ -13,7 +13,7 @@
 EDGE = 16
 SENT = 12
 LANES = 128
-GROUP = 3
+GROUP = 5
 PIECES = 6
 F32 = jnp.float32
 BF16 = jnp.bfloat16

time: 17.4 us -> 17.4 us (level)
  no operation moved by 1% of the time
where the time goes in v6:
time: 17.4 us; the launch traced here: 17.3 us
  Pallas kernels  7.76 us (45%)
  starting transfers between devices  6.48 us (37%)
  local copies, waits for them, and re-layouts  1.66 us (10%)
  waiting for transfers between devices  1.28 us (7%)
    pallas_call x8, Pallas kernels, call(): pl.pallas_call(kernel, out_shape=out_shape, in_specs=[vmem] * len(operand...  6.93 us
    ppermute x3, starting transfers between devices, to_share(): lax.ppermute(values, 'exp', [(i, (i + k) % shares) for i in range(shares)])  6.3 us
    unnamed x14, local copies, waits for them, and re-layouts  1.66 us
    ppermute x3, waiting for transfers between devices, to_share(): lax.ppermute(values, 'exp', [(i, (i + k) % shares) for i in range(shares)])  1.23 us
    pallas_call x1, Pallas kernels, body(): pl.pallas_call(functools.partial(second_coadd_kernel, shares), out_shape=...  0.82 us
  transfers between devices with their start and end apart: 5, of which 2 were waited for; matrix products, arithmetic and copies ran while one was open for 0% of the time, Pallas kernels for 40%

profile of v6, /device:TPU:0, one launch (start us, length us, event | category | flops | bytes accessed | tf_op | source)
XLA Modules:
  0.0 17.3 jit_solution(17568653806174887644)
XLA Ops:
  0.0 0.0 copy-start
  0.0 0.0 copy-start.1
  0.0 1.1 %copy-done.1 = bf16[2,120,1024]{2,1,0:T(8,128)(2,1)S(1)} copy-done((bf16[2,120,1024]{2,1,0:T(8,128)(2,1)S(1)}, bf16[2,120,1024]{2,1,0:T(8,128)(2,1)}, u32[]{:S(2)}) %copy-start.1) | copy-done | bytes 491544
  1.1 0.0 copy-start.2
  1.1 3.0 %collective-permute-start = (bf16[2,120,512]{2,1,0:T(8,128)(2,1)S(1)}, bf16[2,120,512]{2,1,0:T(8,128)(2,1)S(1)}, u32[]{:S(2)}, u32[]{:S(2)}) collective-permute-start(bf16[2,120,512]{2,1,0:T(8,128)(2,1)S(1)} %get-tuple-element.29), channel_id=1, source_target_pairs={{0,1},{1,0},{2,3},{3,2},{4,5},{5,4},{6,7},{7,6},{8,9},{9,8},{10,11... | collective-permute-start | bytes 737288 | tf_op jit(solution)/shard_map/ppermute | solution.py:360
  4.1 0.0 copy-done
  4.1 0.0 copy-start.5
  4.1 0.0 copy-start.6
  4.2 0.0 copy-start.3
  4.2 0.1 collective-permute-start.1
  4.3 0.0 copy-start.4
  4.3 0.1 collective-permute-start.2
  4.4 0.0 copy-done.2
  4.4 0.4 %copy-done.5 = s32[2,2]{1,0:T(2,128)S(1)} copy-done((s32[2,2]{1,0:T(2,128)S(1)}, s32[2,2]{1,0:T(2,128)}, u32[]{:S(2)}) %copy-start.5) | copy-done | bytes 40
  4.8 0.0 copy-done.6
  4.8 0.0 copy-done.3
  4.9 0.1 copy-done.4
  5.0 0.5 %setup.1 = (bf16[9,96,128]{2,1,0:T(8,128)(2,1)S(1)}, bf16[9,32,128]{2,1,0:T(8,128)(2,1)S(1)}, bf16[9,128,128]{2,1,0:T(8,128)(2,1)S(1)}, f32[2,5,8,128]{3,2,1,0:T...) custom-call(bf16[9,2,23]{2,1,0:T(2,128)(2,1)S(1)} %copy-done.3, ...), custom_call_target="tpu_custom_call" | custom-call | flops 500000000 | bytes 1500000 | tf_op jit(solution)/shard_map/setup/pallas_call | solution.py:348
  5.5 0.0 collective-permute-done.1.near
  5.5 2.1 %first.3 = (bf16[2,88,512]{2,1,0:T(8,128)(2,1)S(1)}, bf16[2,5,48,640]{3,2,1,0:T(8,128)(2,1)S(1)}) custom-call(bf16[2,120,1024]{2,1,0:T(8,128)(2,1)S(1)} %copy-done, f32[2,5,8,128]{3,2,1,0:T(8,128)S(1)} %get-tuple-element.33.active, f32[2,120,128]{2,1,0:T(8,128)S(1)} %get-tuple-element.34.covered, bf16[192,128]{1,0:T(8,128)(2,1)S(1)} %get-tuple-element.35.features, ...), custom_call_target="tpu_custom_call" | custom-call | flops 10000000 | bytes 30000 | tf_op jit(solution)/shard_map/first/pallas_call | solution.py:348
  7.6 1.5 %collective-permute-start.4 = (bf16[2,88,512]{2,1,0:T(8,128)(2,1)S(1)}, bf16[2,88,512]{2,1,0:T(8,128)(2,1)S(1)}, u32[]{:S(2)}, u32[]{:S(2)}) collective-permute-start(bf16[2,88,512]{2,1,0:T(8,128)(2,1)S(1)} %get-tuple-element.50), channel_id=1, source_target_pairs={{0,1},{1,0},{2,3},{3,2},{4,5},{5,4},{6,7},{7,6},{8,9},{9,8},{10,11... | collective-permute-start | bytes 540680 | tf_op jit(solution)/shard_map/ppermute | solution.py:360
  9.1 2.0 %first.2 = (bf16[2,88,512]{2,1,0:T(8,128)(2,1)S(1)}, bf16[2,5,48,640]{3,2,1,0:T(8,128)(2,1)S(1)}) custom-call(bf16[2,120,1024]{2,1,0:T(8,128)(2,1)S(1)} %copy-done, f32[2,5,8,128]{3,2,1,0:T(8,128)S(1)} %get-tuple-element.33.active, f32[2,120,128]{2,1,0:T(8,128)S(1)} %get-tuple-element.34.covered, bf16[192,128]{1,0:T(8,128)(2,1)S(1)} %get-tuple-element.35.features, ...), custom_call_target="tpu_custom_call" | custom-call | flops 1500000000 | bytes 4500000 | tf_op jit(solution)/shard_map/first/pallas_call | solution.py:348
  11.1 0.0 collective-permute-done.refs_3_
  11.1 0.0 collective-permute-done.2.far
  11.1 0.9 %second.2 = bf16[2,32,512]{2,1,0:T(8,128)(2,1)S(1)} custom-call(bf16[2,120,1024]{2,1,0:T(8,128)(2,1)S(1)} %copy-done, bf16[24,1024]{1,0:T(8,128)(2,1)S(1)} %collective-permute-done.1.near, bf16[24,1024]{1,0:T(8,128)(2,1)S(1)} %collective-permute-done.2.far, f32[2,120,128]{2,1,0:T(8,128)S(1)} %get-tuple-element.34.covered, ...), custom_call_target="tpu_custom_call" | custom-call | flops 10000000 | bytes 30000 | tf_op jit(solution)/shard_map/second/pallas_call | solution.py:348
  12.1 1.8 %collective-permute-start.3 = (bf16[2,32,512]{2,1,0:T(8,128)(2,1)S(1)}, bf16[2,32,512]{2,1,0:T(8,128)(2,1)S(1)}, u32[]{:S(2)}, u32[]{:S(2)}) collective-permute-start(bf16[2,32,512]{2,1,0:T(8,128)(2,1)S(1)} %second.2), channel_id=1, source_target_pairs={{0,1},{1,0},{2,3},{3,2},{4,5},{5,4},{6,7},{7,6},{8,9},{9,8},{10,11... | collective-permute-start | bytes 196616 | tf_op jit(solution)/shard_map/ppermute | solution.py:360
  13.9 0.9 %second.3.refs_0_ = bf16[2,32,512]{2,1,0:T(8,128)(2,1)S(1)} custom-call(bf16[2,120,1024]{2,1,0:T(8,128)(2,1)S(1)} %copy-done, bf16[24,1024]{1,0:T(8,128)(2,1)S(1)} %collective-permute-done.1.near, bf16[24,1024]{1,0:T(8,128)(2,1)S(1)} %collective-permute-done.2.far, f32[2,120,128]{2,1,0:T(8,128)S(1)} %get-tuple-element.34.covered, ...), custom_call_target="tpu_custom_call" | custom-call | flops 10000000 | bytes 30000 | tf_op jit(solution)/shard_map/second/pallas_call | solution.py:348
  14.8 0.2 %collective-permute-done.4.refs_1_ = bf16[2,88,512]{2,1,0:T(8,128)(2,1)S(1)} collective-permute-done((bf16[2,88,512]{2,1,0:T(8,128)(2,1)S(1)}, bf16[2,88,512]{2,1,0:T(8,128)(2,1)S(1)}, u32[]{:S(2)}, u32[]{:S(2)}) %collective-permute-start.4) | collective-permute-done | bytes 180256 | tf_op jit(solution)/shard_map/ppermute | solution.py:360
  15.0 0.4 %first_coadd.1.refs_4_ = f32[88,512]{1,0:T(8,128)S(1)} custom-call(bf16[2,88,512]{2,1,0:T(8,128)(2,1)S(1)} %get-tuple-element.49.refs_0_, bf16[2,88,512]{2,1,0:T(8,128)(2,1)S(1)} %collective-permute-done.4.refs_1_, bf16[2,120,512]{2,1,0:T(8,128)(2,1)S(1)} %get-tuple-element.47.refs_2_, bf16[2,120,512]{2,1,0:T(8,128)(2,1)S(1)} %collective-permute-done.refs_3_), custom_call_target="tpu_custom_call" | custom-call | flops 10000000 | bytes 30000 | tf_op jit(solution)/shard_map/first_coadd/pallas_call | solution.py:348
  15.4 1.0 %collective-permute-done.3.refs_1_ = bf16[2,32,512]{2,1,0:T(8,128)(2,1)S(1)} collective-permute-done((bf16[2,32,512]{2,1,0:T(8,128)(2,1)S(1)}, bf16[2,32,512]{2,1,0:T(8,128)(2,1)S(1)}, u32[]{:S(2)}, u32[]{:S(2)}) %collective-permute-start.3) | collective-permute-done | bytes 65568 | tf_op jit(solution)/shard_map/ppermute | solution.py:360
  16.5 0.8 %second_coadd.1 = f32[120,512]{1,0:T(8,128)} custom-call(bf16[2,32,512]{2,1,0:T(8,128)(2,1)S(1)} %second.3.refs_0_, bf16[2,32,512]{2,1,0:T(8,128)(2,1)S(1)} %collective-permute-done.3.refs_1_, bf16[2,120,512]{2,1,0:T(8,128)(2,1)S(1)} %get-tuple-element.47.refs_2_, bf16[2,120,512]{2,1,0:T(8,128)(2,1)S(1)} %collective-permute-done.refs_3_, ...), custom_call_target="tpu_custom_call" | custom-call | tf_op jit(solution)/shard_map/second_coadd/pallas_call | solution.py:459
  (2 shorter events, 0.1 us)
Async XLA Ops:
  0.0 4.1 %copy-start = (bf16[2,120,1024]{2,1,0:T(8,128)(2,1)S(1)}, bf16[2,120,1024]{2,1,0:T(8,128)(2,1)}, u32[]{:S(2)}) copy-start(bf16[2,120,1024]{2,1,0:T(8,128)(2,1)} %warped.9) | copy-start | bytes 1474564
  0.0 1.1 %copy-start.1 = (bf16[2,120,1024]{2,1,0:T(8,128)(2,1)S(1)}, bf16[2,120,1024]{2,1,0:T(8,128)(2,1)}, u32[]{:S(2)}) copy-start(bf16[2,120,1024]{2,1,0:T(8,128)(2,1)} %variance.3) | copy-start | bytes 1474564
  1.1 3.3 %copy-start.2 = (f32[2,9,10]{2,0,1:T(2,128)S(1)}, f32[2,9,10]{2,0,1:T(2,128)}, u32[]{:S(2)}) copy-start(f32[2,9,10]{2,0,1:T(2,128)} %param.10) | copy-start | bytes 2164
  1.1 10.0 %collective-permute-start = (bf16[2,120,512]{2,1,0:T(8,128)(2,1)S(1)}, bf16[2,120,512]{2,1,0:T(8,128)(2,1)S(1)}, u32[]{:S(2)}, u32[]{:S(2)}) collective-permute-start(bf16[2,120,512]{2,1,0:T(8,128)(2,1)S(1)} %get-tuple-element.29), channel_id=1, source_target_pairs={{0,1},{1,0},{2,3},{3,2},{4,5},{5,4},{6,7},{7,6},{8,9},{9,8},{10,11... | collective-permute-start | bytes 737288 | tf_op jit(solution)/shard_map/ppermute | solution.py:360
  4.1 0.7 %copy-start.5 = (s32[2,2]{1,0:T(2,128)S(1)}, s32[2,2]{1,0:T(2,128)}, u32[]{:S(2)}) copy-start(s32[2,2]{1,0:T(2,128)} %footprint.1) | copy-start | bytes 52
  4.1 0.7 %copy-start.6 = (s32[2,8]{1,0:T(2,128)S(1)}, s32[2,8]{1,0:T(2,128)}, u32[]{:S(2)}) copy-start(s32[2,8]{1,0:T(2,128)} %masks.1) | copy-start | bytes 196
  4.2 0.7 %copy-start.3 = (bf16[9,2,23]{2,1,0:T(2,128)(2,1)S(1)}, bf16[9,2,23]{2,1,0:T(2,128)(2,1)}, u32[]{:S(2)}) copy-start(bf16[9,2,23]{2,1,0:T(2,128)(2,1)} %taps.1) | copy-start | bytes 2488
  4.2 1.3 %collective-permute-start.1 = (bf16[24,1024]{1,0:T(8,128)(2,1)S(1)}, bf16[24,1024]{1,0:T(8,128)(2,1)S(1)}, u32[]{:S(2)}, u32[]{:S(2)}) collective-permute-start(bf16[24,1024]{1,0:T(8,128)(2,1)S(1)} %get-tuple-element.31), channel_id=1, source_target_pairs={{0,2},{2,0},{4,6},{6,4},{8,10},{10,8},{12,14},{14,12},{16,18},{18,... | collective-permute-start | bytes 147464 | tf_op jit(solution)/shard_map/ppermute | solution.py:367
  4.3 0.7 %copy-start.4 = (s32[2,9]{1,0:T(2,128)S(1)}, s32[2,9]{1,0:T(2,128)}, u32[]{:S(2)}) copy-start(s32[2,9]{1,0:T(2,128)} %degrees.1) | copy-start | bytes 220
  4.3 6.8 %collective-permute-start.2 = (bf16[24,1024]{1,0:T(8,128)(2,1)S(1)}, bf16[24,1024]{1,0:T(8,128)(2,1)S(1)}, u32[]{:S(2)}, u32[]{:S(2)}) collective-permute-start(bf16[24,1024]{1,0:T(8,128)(2,1)S(1)} %get-tuple-element.40), channel_id=1, source_target_pairs={{0,1},{1,0},{2,4},{3,5},{4,2},{5,3},{6,8},{7,9},{8,6},{9,7},{10,12... | collective-permute-start | bytes 147464 | tf_op jit(solution)/shard_map/ppermute | solution.py:375
  7.6 7.4 %collective-permute-start.4 = (bf16[2,88,512]{2,1,0:T(8,128)(2,1)S(1)}, bf16[2,88,512]{2,1,0:T(8,128)(2,1)S(1)}, u32[]{:S(2)}, u32[]{:S(2)}) collective-permute-start(bf16[2,88,512]{2,1,0:T(8,128)(2,1)S(1)} %get-tuple-element.50), channel_id=1, source_target_pairs={{0,1},{1,0},{2,3},{3,2},{4,5},{5,4},{6,7},{7,6},{8,9},{9,8},{10,11... | collective-permute-start | bytes 540680 | tf_op jit(solution)/shard_map/ppermute | solution.py:360
  12.1 4.4 %collective-permute-start.3 = (bf16[2,32,512]{2,1,0:T(8,128)(2,1)S(1)}, bf16[2,32,512]{2,1,0:T(8,128)(2,1)S(1)}, u32[]{:S(2)}, u32[]{:S(2)}) collective-permute-start(bf16[2,32,512]{2,1,0:T(8,128)(2,1)S(1)} %second.2), channel_id=1, source_target_pairs={{0,1},{1,0},{2,3},{3,2},{4,5},{5,4},{6,7},{7,6},{8,9},{9,8},{10,11... | collective-permute-start | bytes 196616 | tf_op jit(solution)/shard_map/ppermute | solution.py:360
